TPU v7x, 32 devices: a whole 2x2x4 slice. The times are simulated.
32 devices in a mesh: dp: 4 (over y, core), ctx: 8 (over z, x).
Axes of the slice: x: 2, y: 2, z: 4, core: 2. Of those that a mesh axis runs over, the one named last changes fastest.
Arguments:
- tokens: bfloat16 [4, 2048, 1024], P('dp', 'ctx'), may hold values from -6 to 6
- cotangent: bfloat16 [4, 2048, 1024], P('dp', 'ctx'), may hold values from -6 to 6
- segments: int32 [4, 2048], P('dp'), may hold values from 0 to 3, as said below
- span_order: int32 [4, 8], P('dp'), may hold values from 0 to 7, as said below
- query_weight: float32 [1024, 2048], P('dp', 'ctx'), may hold values from -0.1875 to 0.1875
- query_moment: float32 [1024, 2048], P('dp', 'ctx'), may hold values from -27.1529 to 27.1529
- query_second: float32 [1024, 2048], P('dp', 'ctx'), may hold values from 106.496 to 434.176
- key_value_weight: float32 [1024, 2048], P('dp', 'ctx'), may hold values from -0.1875 to 0.1875
- key_value_first_moment: float32 [1024, 2048], P('dp', 'ctx'), may hold values from -36.20387 to 36.20387
- key_value_second_moment: float32 [1024, 2048], P('dp', 'ctx'), may hold values from 212.992 to 860.16
- mixing_weight: float32 [2048, 1024], P('dp', 'ctx'), may hold values from -0.75 to 0.75
- mixing_moment: float32 [2048, 1024], P('dp', 'ctx'), may hold values from -9.050967 to 9.050967
- mixing_second: float32 [2048, 1024], P('dp', 'ctx'), may hold values from 9.8304 to 38.5024
- gate_up_weight: float32 [1024, 6144], P('dp', 'ctx'), may hold values from -0.1875 to 0.1875
- gate_up_moment: float32 [1024, 6144], P('dp', 'ctx'), may hold values from -18.101934 to 18.101934
- gate_up_second: float32 [1024, 6144], P('dp', 'ctx'), may hold values from 38.5024 to 155.648
- down_weight: float32 [3072, 1024], P('dp', 'ctx'), may hold values from -0.109375 to 0.109375
- down_moment: float32 [3072, 1024], P('dp', 'ctx'), may hold values from -36.20387 to 36.20387
- down_second: float32 [3072, 1024], P('dp', 'ctx'), may hold values from 155.648 to 622.592
- norm_gains: float32 [2304], replicated, may hold values from 0.5 to 1.5
- gain_moment: float32 [2304], replicated, may hold values from -72.40774 to 72.40774
- gain_second: float32 [2304], replicated, may hold values from 983.04 to 3850.24
Outputs:
- block_output: bfloat16 [4, 2048, 1024], P('dp', 'ctx')
- input_grad: float32 [4, 2048, 1024], P('dp', 'ctx')
- query_weight_new: float32 [1024, 2048], P('dp', 'ctx')
- query_moment_new: float32 [1024, 2048], P('dp', 'ctx')
- query_second_new: float32 [1024, 2048], P('dp', 'ctx')
- keyval_weight_new: float32 [1024, 2048], P('dp', 'ctx')
- keyval_moment_new: float32 [1024, 2048], P('dp', 'ctx')
- keyval_second_new: float32 [1024, 2048], P('dp', 'ctx')
- mixing_weight_new: float32 [2048, 1024], P('dp', 'ctx')
- mixing_moment_new: float32 [2048, 1024], P('dp', 'ctx')
- mixing_second_new: float32 [2048, 1024], P('dp', 'ctx')
- gate_up_weight_new: float32 [1024, 6144], P('dp', 'ctx')
- gate_up_moment_new: float32 [1024, 6144], P('dp', 'ctx')
- gate_up_second_new: float32 [1024, 6144], P('dp', 'ctx')
- down_weight_new: float32 [3072, 1024], P('dp', 'ctx')
- down_moment_new: float32 [3072, 1024], P('dp', 'ctx')
- down_second_new: float32 [3072, 1024], P('dp', 'ctx')
- norm_gains_new: float32 [2304], replicated
- gain_moment_new: float32 [2304], replicated
- gain_second_new: float32 [2304], replicated
Inputs may be any that keep to these rules, and one draw needn't show every extreme that they name: `segments`: read in the order of true positions, a sequence's segment numbers never fall. `span_order`: each row is a permutation of the 8 span numbers; entry c is the span stored in block c of the sequence.
All inputs are finite; a program needn't handle non-finite values.
Results may differ from a plain program's by a relative error of at most 0.024.
Values may be sent and summed in bfloat16 or wider, within the bound.
A program may use at most 320 MiB of HBM per device.

v0:
```python
import functools
import math

import jax
import jax.numpy as jnp
from jax import lax
from jax.sharding import PartitionSpec as P

MODEL_WIDTH = 1024
QUERY_HEADS = 16
KEY_VALUE_HEADS = 8
HEAD_WIDTH = 128
FF = 3072
SEQUENCE_LENGTH = 2048
STEP = 10


norm_eps = 1e-06
rope_base = 1000000.0
beta_first = 0.9
beta_second = 0.95
adam_eps = 1e-08
weight_decay = 0.1
gain_rate = 0.4


def normalized_input(values, gain):
    return values * lax.rsqrt(jnp.mean(values * values, axis=-1, keepdims=True) + norm_eps) * gain


def rotated_output(values, cosine_table, sine_table):
    half_width = values.shape[-1] // 2
    first_half = values[..., :half_width]
    second_half = values[..., half_width:]
    return jnp.concatenate(
        [
            first_half * cosine_table - second_half * sine_table,
            second_half * cosine_table + first_half * sine_table,
        ],
        axis=-1,
    )


def angles_of(positions):
    freq_index = jnp.arange(HEAD_WIDTH // 2, dtype=jnp.float32)
    inverse = rope_base ** (-2.0 * freq_index / HEAD_WIDTH)
    phases = positions.astype(jnp.float32)[..., None] * inverse
    return (jnp.cos(phases), jnp.sin(phases))


def head_norms(query_raw, key_unnormed, query_gain, key_norm_weight, cosine_table, sine_table):
    query_rotated = rotated_output(
        normalized_input(query_raw, query_gain), cosine_table, sine_table
    )
    key_rotated = rotated_output(
        normalized_input(key_unnormed, key_norm_weight), cosine_table, sine_table
    )
    return (query_rotated, key_rotated)


def swiglu(gate_up):
    return jax.nn.silu(gate_up[:, :FF]) * gate_up[:, FF:]


def adamw(weight, moment, second, gradient, rate, decay):
    moment = beta_first * moment + (1.0 - beta_first) * gradient
    second = beta_second * second + (1.0 - beta_second) * gradient * gradient
    scaled = (
        moment
        / (1.0 - beta_first**STEP)
        / (jnp.sqrt(second / (1.0 - beta_second**STEP)) + adam_eps)
    )
    return (weight - rate * (scaled + decay * weight), moment, second)


def rows_product(left_side, right_side):
    return lax.dot_general(
        left_side, right_side, (((0,), (0,)), ((), ())), preferred_element_type=jnp.float32
    )


def times_transposed(left_side, right_side):
    return lax.dot_general(
        left_side, right_side, (((1,), (1,)), ((), ())), preferred_element_type=jnp.float32
    )


def fetch_forward(query_low, keyval_low, mixing_low, gate_up_low, down_low):
    query_rows, keyval_rows, mixing_rows, gate_up_rows, down_rows = (
        lax.all_gather(query_low, "dp", axis=0, tiled=True),
        lax.all_gather(keyval_low, "dp", axis=0, tiled=True),
        lax.all_gather(mixing_low, "dp", axis=0, tiled=True),
        lax.all_gather(gate_up_low, "dp", axis=0, tiled=True),
        lax.all_gather(down_low, "dp", axis=0, tiled=True),
    )
    return (
        lax.all_gather(query_rows, "ctx", axis=1, tiled=True),
        lax.all_gather(keyval_rows, "ctx", axis=1, tiled=True),
        lax.all_gather(mixing_rows, "ctx", axis=1, tiled=True),
        lax.all_gather(gate_up_rows, "ctx", axis=1, tiled=True),
        lax.all_gather(down_rows, "ctx", axis=1, tiled=True),
    )


def owned(left_rows, right_rows):
    gradient = rows_product(left_rows, right_rows)
    partial_sum = lax.psum_scatter(
        gradient.astype(jnp.bfloat16), "ctx", scatter_dimension=1, tiled=True
    )
    result_shard = lax.psum_scatter(partial_sum, "dp", scatter_dimension=0, tiled=True).astype(
        jnp.float32
    )
    return result_shard


def per_device(
    tokens,
    cotangent,
    segments,
    span_order,
    query_weight,
    query_moment,
    query_second,
    key_value_weight,
    key_value_first_moment,
    key_value_second_moment,
    mixing_weight,
    mixing_moment,
    mixing_second,
    gate_up_weight,
    gate_up_moment,
    gate_up_second,
    down_weight,
    down_moment,
    down_second,
    norm_gains,
    gain_moment,
    gain_second,
):
    sequence_count = tokens.shape[0]
    span_length = tokens.shape[1]
    count_of_rows = sequence_count * span_length
    ctx_index = lax.axis_index("ctx")
    heads_per_group = QUERY_HEADS // KEY_VALUE_HEADS
    scale_factor = HEAD_WIDTH ** (-0.5)
    query_low_w = query_weight.astype(jnp.bfloat16)
    keyval_low_w = key_value_weight.astype(jnp.bfloat16)
    mixing_low_w = mixing_weight.astype(jnp.bfloat16)
    gate_up_low_w = gate_up_weight.astype(jnp.bfloat16)
    down_low_w = down_weight.astype(jnp.bfloat16)
    query_full, keyval_full, mixing_full, gate_up_full, down_full = fetch_forward(
        query_low_w, keyval_low_w, mixing_low_w, gate_up_low_w, down_low_w
    )
    offsets = jnp.arange(SEQUENCE_LENGTH, dtype=jnp.int32) % span_length
    positions = jnp.repeat(span_order, span_length, axis=1) * span_length + offsets
    own_start = ctx_index * span_length
    own_positions = lax.dynamic_slice_in_dim(positions, own_start, span_length, 1)
    own_segments = lax.dynamic_slice_in_dim(segments, own_start, span_length, 1)
    permitted_mask = (own_segments[:, :, None] == segments[:, None, :]) & (
        positions[:, None, :] <= own_positions[:, :, None]
    )
    permitted_mask = permitted_mask[:, None, None, :, :]
    cosine_table, sine_table = angles_of(own_positions)
    cosine_table = cosine_table[:, :, None, :]
    sine_table = sine_table[:, :, None, :]
    attn_gain = norm_gains[:MODEL_WIDTH]
    mlp_gain = norm_gains[MODEL_WIDTH : 2 * MODEL_WIDTH]
    query_gain = norm_gains[2 * MODEL_WIDTH : 2 * MODEL_WIDTH + HEAD_WIDTH]
    key_norm_weight = norm_gains[2 * MODEL_WIDTH + HEAD_WIDTH :]
    inputs = tokens.astype(jnp.float32).reshape(count_of_rows, MODEL_WIDTH)
    normed_one = normalized_input(inputs, attn_gain).astype(jnp.bfloat16)
    query_raw = jnp.dot(normed_one, query_full, preferred_element_type=jnp.float32).reshape(
        sequence_count, span_length, QUERY_HEADS, HEAD_WIDTH
    )
    key_value_projected = jnp.dot(normed_one, keyval_full, preferred_element_type=jnp.float32)
    key_unnormed = key_value_projected[:, : KEY_VALUE_HEADS * HEAD_WIDTH].reshape(
        sequence_count, span_length, KEY_VALUE_HEADS, HEAD_WIDTH
    )
    value_bfloat = key_value_projected[:, KEY_VALUE_HEADS * HEAD_WIDTH :].astype(jnp.bfloat16)
    head_fn = functools.partial(head_norms, cosine_table=cosine_table, sine_table=sine_table)
    query_rotated, key_rotated = head_fn(query_raw, key_unnormed, query_gain, key_norm_weight)
    query_groups = query_rotated.astype(jnp.bfloat16).reshape(
        sequence_count, span_length, KEY_VALUE_HEADS, heads_per_group, HEAD_WIDTH
    )
    key_bfloat = key_rotated.astype(jnp.bfloat16).reshape(
        sequence_count, span_length, KEY_VALUE_HEADS * HEAD_WIDTH
    )
    gathered_keys, gathered_values = (
        lax.all_gather(key_bfloat, "ctx", axis=1, tiled=True),
        lax.all_gather(
            value_bfloat.reshape(sequence_count, span_length, KEY_VALUE_HEADS * HEAD_WIDTH),
            "ctx",
            axis=1,
            tiled=True,
        ),
    )
    key_head_split = gathered_keys.reshape(
        sequence_count, SEQUENCE_LENGTH, KEY_VALUE_HEADS, HEAD_WIDTH
    )
    value_head_split = gathered_values.reshape(
        sequence_count, SEQUENCE_LENGTH, KEY_VALUE_HEADS, HEAD_WIDTH
    )

    def attention_scores():
        raw_scores = (
            jnp.einsum(
                "sqhgd,skhd->shgqk",
                query_groups,
                key_head_split,
                preferred_element_type=jnp.float32,
            )
            * scale_factor
        )
        return jnp.where(permitted_mask, raw_scores, -1e30)

    scores = attention_scores()
    log_total = jax.nn.logsumexp(scores, axis=-1, keepdims=True)
    probs_low = jnp.exp(scores - log_total).astype(jnp.bfloat16)
    attention_output = jnp.einsum(
        "shgqk,skhd->sqhgd", probs_low, value_head_split, preferred_element_type=jnp.float32
    )
    attended_low = attention_output.reshape(count_of_rows, QUERY_HEADS * HEAD_WIDTH).astype(
        jnp.bfloat16
    )
    middle = inputs + jnp.dot(attended_low, mixing_full, preferred_element_type=jnp.float32)
    normed_two = normalized_input(middle, mlp_gain).astype(jnp.bfloat16)
    gate_up = jnp.dot(normed_two, gate_up_full, preferred_element_type=jnp.float32)
    hidden_low = swiglu(gate_up).astype(jnp.bfloat16)
    result = middle + jnp.dot(hidden_low, down_full, preferred_element_type=jnp.float32)
    block_output = result.astype(jnp.bfloat16).reshape(sequence_count, span_length, MODEL_WIDTH)
    query_back, keyval_back, mixing_back, gate_up_back, down_back = (
        query_full,
        keyval_full,
        mixing_full,
        gate_up_full,
        down_full,
    )
    grad_rows = cotangent.reshape(count_of_rows, MODEL_WIDTH)
    down_new = adamw(
        down_weight,
        down_moment,
        down_second,
        owned(hidden_low, grad_rows),
        2.0 / math.sqrt(FF),
        weight_decay,
    )
    hidden_grad = times_transposed(grad_rows, down_back)
    unused_value, swiglu_back = jax.vjp(swiglu, gate_up)
    gate_up_grad = swiglu_back(hidden_grad)[0].astype(jnp.bfloat16)
    gate_up_new = adamw(
        gate_up_weight,
        gate_up_moment,
        gate_up_second,
        owned(normed_two, gate_up_grad),
        2.0 / math.sqrt(MODEL_WIDTH),
        weight_decay,
    )
    normed_two_grad = times_transposed(gate_up_grad, gate_up_back)
    unused_norm, norm_two_back = jax.vjp(normalized_input, middle, mlp_gain)
    middle_part, mlp_gain_grad = norm_two_back(normed_two_grad)
    middle_grad = grad_rows.astype(jnp.float32) + middle_part
    middle_low = middle_grad.astype(jnp.bfloat16)
    mixing_new = adamw(
        mixing_weight,
        mixing_moment,
        mixing_second,
        owned(attended_low, middle_low),
        2.0 / math.sqrt(QUERY_HEADS * HEAD_WIDTH // 32),
        weight_decay,
    )
    attended_grad = (
        times_transposed(middle_low, mixing_back)
        .astype(jnp.bfloat16)
        .reshape(sequence_count, span_length, KEY_VALUE_HEADS, heads_per_group, HEAD_WIDTH)
    )
    scores = attention_scores()
    probs_full = jnp.exp(scores - log_total)
    probs_again = probs_full.astype(jnp.bfloat16)
    prob_grad = jnp.einsum(
        "sqhgd,skhd->shgqk", attended_grad, value_head_split, preferred_element_type=jnp.float32
    )
    row_delta = jnp.sum(probs_full * prob_grad, axis=-1, keepdims=True)
    score_grad = (probs_full * (prob_grad - row_delta)).astype(jnp.bfloat16)
    query_rot_grad = (
        jnp.einsum(
            "shgqk,skhd->sqhgd", score_grad, key_head_split, preferred_element_type=jnp.float32
        )
        * scale_factor
    )
    key_portion = (
        jnp.einsum(
            "shgqk,sqhgd->skhd", score_grad, query_groups, preferred_element_type=jnp.float32
        )
        * scale_factor
    )
    value_portion = jnp.einsum(
        "shgqk,sqhgd->skhd", probs_again, attended_grad, preferred_element_type=jnp.float32
    )
    key_gradient_total, value_gradient_total = (
        lax.psum_scatter(
            key_portion.reshape(sequence_count, SEQUENCE_LENGTH, KEY_VALUE_HEADS * HEAD_WIDTH),
            "ctx",
            scatter_dimension=1,
            tiled=True,
        ),
        lax.psum_scatter(
            value_portion.reshape(sequence_count, SEQUENCE_LENGTH, KEY_VALUE_HEADS * HEAD_WIDTH),
            "ctx",
            scatter_dimension=1,
            tiled=True,
        ),
    )
    unused_heads, heads_back = jax.vjp(
        head_fn, query_raw, key_unnormed, query_gain, key_norm_weight
    )
    query_raw_grad, key_unnormed_gradient, query_gain_grad, key_gain_grad = heads_back(
        (
            query_rot_grad.reshape(sequence_count, span_length, QUERY_HEADS, HEAD_WIDTH),
            key_gradient_total.reshape(sequence_count, span_length, KEY_VALUE_HEADS, HEAD_WIDTH),
        )
    )
    query_grad = query_raw_grad.reshape(count_of_rows, QUERY_HEADS * HEAD_WIDTH).astype(
        jnp.bfloat16
    )
    keyval_grad = jnp.concatenate(
        [
            key_unnormed_gradient.reshape(count_of_rows, KEY_VALUE_HEADS * HEAD_WIDTH),
            value_gradient_total.reshape(count_of_rows, KEY_VALUE_HEADS * HEAD_WIDTH),
        ],
        axis=1,
    ).astype(jnp.bfloat16)
    query_new = adamw(
        query_weight,
        query_moment,
        query_second,
        owned(normed_one, query_grad),
        2.0 / math.sqrt(MODEL_WIDTH),
        weight_decay,
    )
    keyval_new = adamw(
        key_value_weight,
        key_value_first_moment,
        key_value_second_moment,
        owned(normed_one, keyval_grad),
        2.0 / math.sqrt(MODEL_WIDTH),
        weight_decay,
    )
    normed_one_grad = times_transposed(query_grad, query_back) + times_transposed(
        keyval_grad, keyval_back
    )
    unused_first, norm_one_back = jax.vjp(normalized_input, inputs, attn_gain)
    input_part, attn_gain_grad = norm_one_back(normed_one_grad)
    input_grad = (middle_grad + input_part).reshape(sequence_count, span_length, MODEL_WIDTH)
    gain_terms = jnp.concatenate([attn_gain_grad, mlp_gain_grad, query_gain_grad, key_gain_grad])
    gain_total = lax.psum(gain_terms, ("dp", "ctx"))
    gains_new = adamw(norm_gains, gain_moment, gain_second, gain_total, gain_rate, 0.0)
    return (
        block_output,
        input_grad,
        query_new[0],
        query_new[1],
        query_new[2],
        keyval_new[0],
        keyval_new[1],
        keyval_new[2],
        mixing_new[0],
        mixing_new[1],
        mixing_new[2],
        gate_up_new[0],
        gate_up_new[1],
        gate_up_new[2],
        down_new[0],
        down_new[1],
        down_new[2],
        gains_new[0],
        gains_new[1],
        gains_new[2],
    )


def solution(mesh):
    in_specs = (
        P("dp", "ctx", None),
        P("dp", "ctx", None),
        P("dp", None),
        P("dp", None),
        P("dp", "ctx"),
        P("dp", "ctx"),
        P("dp", "ctx"),
        P("dp", "ctx"),
        P("dp", "ctx"),
        P("dp", "ctx"),
        P("dp", "ctx"),
        P("dp", "ctx"),
        P("dp", "ctx"),
        P("dp", "ctx"),
        P("dp", "ctx"),
        P("dp", "ctx"),
        P("dp", "ctx"),
        P("dp", "ctx"),
        P("dp", "ctx"),
        P(),
        P(),
        P(),
    )
    out_specs = (
        P("dp", "ctx", None),
        P("dp", "ctx", None),
        P("dp", "ctx"),
        P("dp", "ctx"),
        P("dp", "ctx"),
        P("dp", "ctx"),
        P("dp", "ctx"),
        P("dp", "ctx"),
        P("dp", "ctx"),
        P("dp", "ctx"),
        P("dp", "ctx"),
        P("dp", "ctx"),
        P("dp", "ctx"),
        P("dp", "ctx"),
        P("dp", "ctx"),
        P("dp", "ctx"),
        P("dp", "ctx"),
        P(),
        P(),
        P(),
    )
    return jax.shard_map(
        per_device, mesh=mesh, in_specs=in_specs, out_specs=out_specs, check_vma=False
    )
```

profile of v0, /device:TPU:0, one launch (start us, length us, event | category | flops | bytes accessed | tf_op | source)
XLA Modules:
  0.0 1836.6 jit_solution(16891370168377049141)
XLA Ops:
  28.5 64.9 %all-gather.10.cloned.1.call-done = bf16[1024,2048]{1,0:T(8,128)(2,1)} async-done(((bf16[1024,256]{1,0:T(8,128)(2,1)}), bf16[1024,2048]{1,0:T(8,128)(2,1)}) %all-gather.10.cloned.1.call-update) | async-done | bytes 4194320 | tf_op jit(solution)/shard_map/all_gather | solution.py:98
  127.9 65.5 %all-gather.14.cloned.1.call-done = bf16[1024,2048]{1,0:T(8,128)(2,1)} async-done(((bf16[1024,256]{1,0:T(8,128)(2,1)}), bf16[1024,2048]{1,0:T(8,128)(2,1)}) %all-gather.14.cloned.1.call-update) | async-done | bytes 4194320 | tf_op jit(solution)/shard_map/all_gather | solution.py:97
  202.9 64.7 %all-gather.24.cloned.1.call-done = bf16[2048,1024]{1,0:T(8,128)(2,1)} async-done(((bf16[256,1024]{1,0:T(8,128)(2,1)}), bf16[2048,1024]{1,0:T(8,128)(2,1)}) %all-gather.24.cloned.1.call-update) | async-done | bytes 4194320 | tf_op jit(solution)/shard_map/all_gather | solution.py:190
  272.8 70.5 %all-gather.12.cloned.1.call-done = bf16[1,2048,1024]{1,2,0:T(8,128)(2,1)} async-done(((bf16[1,256,1024]{1,2,0:T(8,128)(2,1)}), bf16[1,2048,1024]{1,2,0:T(8,128)(2,1)}) %all-gather.12.cloned.1.call-update) | async-done | bytes 4194320 | tf_op jit(solution)/shard_map/all_gather | solution.py:189
  343.3 16.7 fusion.4
  360.0 14.4 exponential_reduce_fusion
  374.4 17.0 fusion.18
  391.4 27.0 %all-gather.16.cloned.1.call-done = bf16[2048,1024]{1,0:T(8,128)(2,1)} async-done(((bf16[2048,128]{1,0:T(8,128)(2,1)}), bf16[2048,1024]{1,0:T(8,128)(2,1)}) %all-gather.16.cloned.1.call-update) | async-done | bytes 4194320 | tf_op jit(solution)/shard_map/all_gather | solution.py:99
  422.0 173.1 %all-gather.20.cloned.1.call-done = bf16[1024,6144]{1,0:T(8,128)(2,1)} async-done(((bf16[1024,768]{1,0:T(8,128)(2,1)}), bf16[1024,6144]{1,0:T(8,128)(2,1)}) %all-gather.20.cloned.1.call-update) | async-done | bytes 12582928 | tf_op jit(solution)/shard_map/all_gather | solution.py:100
  605.5 89.8 %all-gather.22.cloned.1.call-done = bf16[3072,1024]{1,0:T(8,128)(2,1)} async-done(((bf16[3072,128]{1,0:T(8,128)(2,1)}), bf16[3072,1024]{1,0:T(8,128)(2,1)}) %all-gather.22.cloned.1.call-update) | async-done | bytes 6291472 | tf_op jit(solution)/shard_map/all_gather | solution.py:101
  725.0 25.7 %fusion = (f32[8,2,256]{2,1,0:T(2,128)S(1)}, f32[8,2048,256,2]{2,1,3,0:T(8,128)}) fusion(f32[8,2048,256,2]{2,1,3,0:T(8,128)} %get-tuple-element.72, f32[8,2,256]{2,1,0:T(2,128)S(1)} %log_add_fusion, pred[256,2048]{0,1:T(8,128)(4,1)S(1)} %compare_and_fusion, bf16[256,8,2,128]{0,3,2,1:T(8,128)(2,1)S(1)} %bitcast.242, bf16[2048,8,128,1]{2,1,0,3:T(8,128)(2,1)} %bitcast.232), kind=kOutput, calls=%fused_computation.3 | convolution fusion | flops 2189422592 | bytes 72908800 | tf_op jit(solution)/shard_map/sqhgd,skhd->shgqk/dot_general | solution.py:279
  750.8 28.3 %fusion.6 = bf16[8,2,256,2048]{2,3,1,0:T(8,128)(2,1)} fusion(f32[8,2048,256,2]{2,1,3,0:T(8,128)} %get-tuple-element.77, f32[8,2048,256,2]{2,1,3,0:T(8,128)} %get-tuple-element.72, f32[8,2,256]{2,1,0:T(2,128)S(1)} %get-tuple-element.76, f32[8,2,256]{2,1,0:T(2,128)S(1)} %log_add_fusion, pred[256,2048]{0,1:T(8,128)(4,1)S(1)} %compare_and_fusion), kind=kLoop, calls=%fused_computation.11 | loop fusion | flops 50331648 | bytes 84443136 | tf_op jit(solution)/shard_map/reshape.63
  791.4 17.8 fusion.69
  865.3 72.7 %reduce-scatter.17.cloned.1.call-done = f32[1,256,1024]{1,2,0:T(8,128)} async-done(((f32[1,2048,1024]{1,2,0:T(8,128)}), f32[1,256,1024]{1,2,0:T(8,128)}) %reduce-scatter.17.cloned.1.call-update) | async-done | bytes 1048592 | tf_op jit(solution)/shard_map/reduce_scatter | solution.py:300
  950.0 140.3 %reduce-scatter.19.cloned.1.call-done = f32[1,256,1024]{1,2,0:T(8,128)} async-done(((f32[1,2048,1024]{1,2,0:T(8,128)}), f32[1,256,1024]{1,2,0:T(8,128)}) %reduce-scatter.19.cloned.1.call-update) | async-done | bytes 1048592 | tf_op jit(solution)/shard_map/reduce_scatter | solution.py:306
  1104.7 76.2 %reduce-scatter.37.cloned.1.call-done = bf16[128,2048]{1,0:T(8,128)(2,1)} async-done(((bf16[1024,2048]{1,0:T(8,128)(2,1)}), bf16[128,2048]{1,0:T(8,128)(2,1)}) %reduce-scatter.37.cloned.1.call-update) | async-done | bytes 524304
  1182.9 90.1 %reduce-scatter.21.cloned.1.call-done = bf16[1024,256]{1,0:T(8,128)(2,1)} async-done(((bf16[1024,2048]{1,0:T(8,128)(2,1)}), bf16[1024,256]{1,0:T(8,128)(2,1)}) %reduce-scatter.21.cloned.1.call-update) | async-done | bytes 524304 | tf_op jit(solution)/shard_map/reduce_scatter | solution.py:107
  1273.1 121.2 %reduce-scatter.39.cloned.1.call-done = bf16[128,3072]{1,0:T(8,128)(2,1)} async-done(((bf16[1024,3072]{1,0:T(8,128)(2,1)}), bf16[128,3072]{1,0:T(8,128)(2,1)}) %reduce-scatter.39.cloned.1.call-update) | async-done | bytes 786448
  1396.7 88.8 %reduce-scatter.25.cloned.1.call-done = bf16[1024,256]{1,0:T(8,128)(2,1)} async-done(((bf16[1024,2048]{1,0:T(8,128)(2,1)}), bf16[1024,256]{1,0:T(8,128)(2,1)}) %reduce-scatter.25.cloned.1.call-update) | async-done | bytes 524304 | tf_op jit(solution)/shard_map/reduce_scatter | solution.py:107
  1485.5 211.0 %reduce-scatter.31.cloned.1.call-done = bf16[1024,768]{1,0:T(8,128)(2,1)} async-done(((bf16[1024,6144]{1,0:T(8,128)(2,1)}), bf16[1024,768]{1,0:T(8,128)(2,1)}) %reduce-scatter.31.cloned.1.call-update) | async-done | bytes 1572880 | tf_op jit(solution)/shard_map/reduce_scatter | solution.py:107
  1706.6 13.8 reduce-scatter.29.cloned.1.call-done
  1722.5 21.9 %reduce-scatter.23.cloned.1.call-done = bf16[256,256]{1,0:T(8,128)(2,1)} async-done(((bf16[1024,256]{1,0:T(8,128)(2,1)}), bf16[256,256]{1,0:T(8,128)(2,1)}) %reduce-scatter.23.cloned.1.call-update) | async-done | bytes 131088 | tf_op jit(solution)/shard_map/reduce_scatter | solution.py:110
  1746.6 24.2 %reduce-scatter.35.cloned.1.call-done = bf16[768,128]{1,0:T(8,128)(2,1)} async-done(((bf16[3072,128]{1,0:T(8,128)(2,1)}), bf16[768,128]{1,0:T(8,128)(2,1)}) %reduce-scatter.35.cloned.1.call-update) | async-done | bytes 196624 | tf_op jit(solution)/shard_map/reduce_scatter | solution.py:110
  1778.3 39.6 %psum.7 = f32[2304]{0:T(1024)S(1)} all-reduce(f32[2304]{0:T(1024)S(1)} %pad_maximum_fusion.7), channel_id=1, replica_groups=mesh['dp'=4,'ctx'=8] {'dp','ctx'}, use_global_device_ids=true, to_apply=%region_27.28 | all-reduce | flops 2304 | bytes 18432 | tf_op jit(solution)/shard_map/psum | solution.py:355
  (268 shorter events, 245.8 us)
Async XLA Ops:
  7.2 86.2 %all-gather.10.cloned.1.call-start = ((), (), s32[]{:S(2)}) async-start(), calls=%async_computation.12 | async-start | bytes 4718592 | tf_op jit(solution)/shard_map/all_gather | solution.py:98
  17.4 98.8 %all-gather.18.cloned.1.call-start = ((), (), s32[]{:S(2)}) async-start(), calls=%async_computation.16 | async-start | bytes 1966080 | tf_op jit(solution)/shard_map/all_gather | solution.py:93
  19.4 174.0 %all-gather.14.cloned.1.call-start = ((), (), s32[]{:S(2)}) async-start(), calls=%async_computation.14 | async-start | bytes 4718592 | tf_op jit(solution)/shard_map/all_gather | solution.py:97
  28.2 239.3 %all-gather.24.cloned.1.call-start = ((), (), s32[]{:S(2)}) async-start(), calls=%async_computation.29 | async-start | bytes 4718592 | tf_op jit(solution)/shard_map/all_gather | solution.py:190
  28.4 164.9 %copy-start.48 = (f32[256]{0:T(256)}, f32[256]{0:T(256)S(1)}, u32[]{:S(2)}) copy-start(f32[256]{0:T(256)S(1)} %fusion.81) | copy-start | bytes 3076
  99.2 244.1 %all-gather.12.cloned.1.call-start = ((), (), s32[]{:S(2)}) async-start(), calls=%async_computation.13 | async-start | bytes 4718592 | tf_op jit(solution)/shard_map/all_gather | solution.py:189
  106.7 311.7 %all-gather.16.cloned.1.call-start = ((), (), s32[]{:S(2)}) async-start(), calls=%async_computation.15 | async-start | bytes 4718592 | tf_op jit(solution)/shard_map/all_gather | solution.py:99
  116.1 479.0 %all-gather.20.cloned.1.call-start = ((), (), s32[]{:S(2)}) async-start(), calls=%async_computation.17 | async-start | bytes 14155776 | tf_op jit(solution)/shard_map/all_gather | solution.py:100
  116.8 578.4 %all-gather.22.cloned.1.call-start = ((), (), s32[]{:S(2)}) async-start(), calls=%async_computation.18 | async-start | bytes 7077888 | tf_op jit(solution)/shard_map/all_gather | solution.py:101
  126.1 811.8 %reduce-scatter.17.cloned.1.call-start = ((), (), s32[]{:S(2)}) async-start(), calls=%async_computation.19 | async-start | bytes 9437184 | tf_op jit(solution)/shard_map/reduce_scatter | solution.py:300
  391.4 214.1 %copy-start.26 = (bf16[8,128,2,256]{3,1,2,0:T(8,128)(2,1)}, bf16[8,128,2,256]{3,1,2,0:T(8,128)(2,1)S(1)}, u32[]{:S(2)}) copy-start(bf16[8,128,2,256]{3,1,2,0:T(8,128)(2,1)S(1)} %fusion.18) | copy-start | bytes 3145732
  422.0 295.0 %copy-start.7 = (f32[256,1024]{1,0:T(8,128)}, f32[256,1024]{1,0:T(8,128)S(1)}, u32[]{:S(2)}) copy-start(f32[256,1024]{1,0:T(8,128)S(1)} %get-tuple-element.74) | copy-start | bytes 3145732
  790.2 300.1 %reduce-scatter.19.cloned.1.call-start = ((), (), s32[]{:S(2)}) async-start(), calls=%async_computation.20 | async-start | bytes 9437184 | tf_op jit(solution)/shard_map/reduce_scatter | solution.py:306
  809.2 371.6 %reduce-scatter.37.cloned.1.call-start = ((), (), s32[]{:S(2)}) async-start(), calls=%async_computation.30 | async-start | bytes 4718592
  820.4 452.7 %reduce-scatter.21.cloned.1.call-start = ((), (), s32[]{:S(2)}) async-start(), calls=%async_computation.21 | async-start | bytes 4718592 | tf_op jit(solution)/shard_map/reduce_scatter | solution.py:107
  850.2 544.1 %reduce-scatter.39.cloned.1.call-start = ((), (), s32[]{:S(2)}) async-start(), calls=%async_computation.31 | async-start | bytes 7077888
  865.0 620.5 %reduce-scatter.25.cloned.1.call-start = ((), (), s32[]{:S(2)}) async-start(), calls=%async_computation.23 | async-start | bytes 4718592 | tf_op jit(solution)/shard_map/reduce_scatter | solution.py:107
  1095.1 601.4 %reduce-scatter.31.cloned.1.call-start = ((), (), s32[]{:S(2)}) async-start(), calls=%async_computation.26 | async-start | bytes 14155776 | tf_op jit(solution)/shard_map/reduce_scatter | solution.py:107
  1104.6 591.9 %copy-start.18 = (bf16[1,256,16,128]{3,2,1,0:T(8,128)(2,1)S(1)}, bf16[1,256,16,128]{3,2,1,0:T(8,128)(2,1)}, u32[]{:S(2)}) copy-start(bf16[1,256,16,128]{3,2,1,0:T(8,128)(2,1)} %copy-done.17) | copy-start | bytes 3145732
  1104.6 615.8 %reduce-scatter.29.cloned.1.call-start = ((), (), s32[]{:S(2)}) async-start(), calls=%async_computation.25 | async-start | bytes 655360 | tf_op jit(solution)/shard_map/reduce_scatter | solution.py:110
  1182.9 561.5 %reduce-scatter.23.cloned.1.call-start = ((), (), s32[]{:S(2)}) async-start(), calls=%async_computation.22 | async-start | bytes 655360 | tf_op jit(solution)/shard_map/reduce_scatter | solution.py:110
  1273.1 497.8 %reduce-scatter.35.cloned.1.call-start = ((), (), s32[]{:S(2)}) async-start(), calls=%async_computation.28 | async-start | bytes 983040 | tf_op jit(solution)/shard_map/reduce_scatter | solution.py:110
  1396.7 424.4 %reduce-scatter.27.cloned.1.call-start = ((), (), s32[]{:S(2)}) async-start(), calls=%async_computation.24 | async-start | bytes 655360 | tf_op jit(solution)/shard_map/reduce_scatter | solution.py:110
  1485.5 340.5 %reduce-scatter.33.cloned.1.call-start = ((), (), s32[]{:S(2)}) async-start(), calls=%async_computation.27 | async-start | bytes 1966080 | tf_op jit(solution)/shard_map/reduce_scatter | solution.py:110
  (59 other events, 1867.2 us)
Sparse Core Ops, SparseCore 0:
  17.5 75.8 all-gather.9
  95.6 18.5 all-gather.17
  116.2 77.1 all-gather.13
  195.9 71.5 all-gather.23
  270.0 73.2 all-gather.11
  345.2 73.1 all-gather.15
  420.6 174.3 all-gather.19
  597.1 98.1 all-gather.21
  790.3 147.5 reduce-scatter.16
  941.8 148.3 reduce-scatter.18
  1093.9 86.8 reduce-scatter.36
  1184.7 88.2 reduce-scatter.20
  1276.6 117.6 reduce-scatter.38
  1397.8 87.5 reduce-scatter.24
  1489.3 207.1 reduce-scatter.30
  1699.6 20.7 reduce-scatter.28
  1722.7 21.6 reduce-scatter.22
  1747.5 23.2 reduce-scatter.34
  1773.3 21.7 reduce-scatter.26
  1797.7 28.2 reduce-scatter.32
where the time goes:
time: 1840 us
  waiting for transfers between devices  1420 us (77%)
  matrix products  185 us (10%)
  other arithmetic  88.1 us (5%)
  blocking collectives  73.9 us (4%)
  local copies, waits for them, and re-layouts  53.1 us (3%)
    reduce_scatter x3, waiting for transfers between devices, owned(): lax.psum_scatter(gradient.astype(jnp.bfloat16), 'ctx', scatter_dimension=...  390 us
    unnamed x22, waiting for transfers between devices  198 us
    all_gather x1, waiting for transfers between devices, fetch_forward(): lax.all_gather(gate_up_rows, 'ctx', axis=1, tiled=True)  173 us
    reduce_scatter x1, waiting for transfers between devices, per_device(): lax.psum_scatter(value_portion.reshape(sequence_count, SEQUENCE_LENGTH, K...  140 us
    all_gather x1, waiting for transfers between devices, fetch_forward(): lax.all_gather(down_rows, 'ctx', axis=1, tiled=True)  89.8 us
    reduce_scatter x1, waiting for transfers between devices, per_device(): lax.psum_scatter(key_portion.reshape(sequence_count, SEQUENCE_LENGTH, KEY...  72.7 us
    all_gather x1, waiting for transfers between devices, per_device(): lax.all_gather(key_bfloat, 'ctx', axis=1, tiled=True)  70.5 us
    all_gather x1, waiting for transfers between devices, fetch_forward(): lax.all_gather(query_rows, 'ctx', axis=1, tiled=True)  65.5 us
  transfers between devices with their start and end apart: 20, of which 18 were waited for; matrix products, arithmetic and copies ran while one was open for 12% of the time, Pallas kernels for 0%

commit v1 on v0

--- a/solution.py
+++ b/solution.py
@@ -4,6 +4,8 @@
 import jax
 import jax.numpy as jnp
 from jax import lax
+from jax.experimental import pallas as pl
+from jax.experimental.pallas import tpu as pltpu
 from jax.sharding import PartitionSpec as P
 
 MODEL_WIDTH = 1024
@@ -12,6 +14,7 @@
 HEAD_WIDTH = 128
 FF = 3072
 SEQUENCE_LENGTH = 2048
+SEQUENCES = 4
 STEP = 10
 
 
@@ -113,7 +116,7 @@
     return result_shard
 
 
-def per_device(
+def wide_device(
     tokens,
     cotangent,
     segments,
@@ -378,6 +381,422 @@
     )
 
 
+def exchange_pairs(count):
+    half = count // 2
+    first = [(s, 2 * s) for s in range(half)] + [(half + s, 2 * s + 1) for s in range(half)]
+    second = [(s, 2 * s + 1) for s in range(half)] + [(half + s, 2 * s) for s in range(half)]
+    return first, second
+
+
+def pair_columns(shard, ctx_index, count):
+    half = shard.shape[1] // 2
+    low, high = shard[:, :half], shard[:, half:]
+    first, second = exchange_pairs(count)
+    is_left = ctx_index < count // 2
+    got_first = lax.ppermute(jnp.where(is_left, low, high), "ctx", first)
+    got_second = lax.ppermute(jnp.where(is_left, high, low), "ctx", second)
+    even = ctx_index % 2 == 0
+    return jnp.concatenate(
+        [jnp.where(even, got_first, got_second), jnp.where(even, got_second, got_first)], axis=1
+    )
+
+
+def unpair_columns(paired, ctx_index, count):
+    half = paired.shape[1] // 2
+    left, right = paired[:, :half], paired[:, half:]
+    first, second = exchange_pairs(count)
+    even = ctx_index % 2 == 0
+    got_first = lax.ppermute(jnp.where(even, left, right), "ctx", [(b, a) for a, b in first])
+    got_second = lax.ppermute(jnp.where(even, right, left), "ctx", [(b, a) for a, b in second])
+    is_left = ctx_index < count // 2
+    return jnp.concatenate(
+        [jnp.where(is_left, got_first, got_second), jnp.where(is_left, got_second, got_first)],
+        axis=1,
+    )
+
+
+def gather(values, axis_name):
+    return lax.all_gather(values, axis_name, axis=0, tiled=True)
+
+
+def scatter(values, axis_name):
+    return lax.psum_scatter(
+        values.astype(jnp.bfloat16), axis_name, scatter_dimension=0, tiled=True
+    ).astype(jnp.float32)
+
+
+def attend_kernel(order_ref, start_ref, query_ref, key_ref, value_ref, out_ref, sum_ref):
+    block = pl.program_id(0)
+    blocks = pl.num_programs(0)
+    span = query_ref.shape[0]
+    width = HEAD_WIDTH
+    factor = HEAD_WIDTH ** (-0.5) * math.log2(math.e)
+    query = jnp.concatenate([query_ref[:, :width], query_ref[:, width:]], axis=0)
+    own = order_ref[block]
+    rows = own * span + lax.broadcasted_iota(jnp.int32, (span, span), 0)
+    columns = lax.broadcasted_iota(jnp.int32, (span, span), 1)
+    starts = start_ref[...]
+
+    def one_span(turn, total):
+        place = pl.multiple_of(order_ref[blocks + turn] * span, span)
+        scores = lax.dot_general(
+            query,
+            key_ref[pl.ds(place, span), :],
+            (((1,), (1,)), ((), ())),
+            preferred_element_type=jnp.float32,
+        )
+        at = columns + turn * span
+        allowed = (at <= rows) & (at >= starts)
+        allowed = jnp.concatenate([allowed, allowed], axis=0)
+        terms = jnp.where(allowed, jnp.exp2(scores * factor), 0.0).astype(jnp.bfloat16)
+        return total + jnp.dot(
+            terms, value_ref[pl.ds(place, span), :], preferred_element_type=jnp.float32
+        )
+
+    total = lax.fori_loop(
+        order_ref[2 * blocks + block],
+        own + 1,
+        one_span,
+        jnp.zeros((2 * span, 2 * width), jnp.float32),
+    )
+    mixed = total[:, :width] / total[:, width:]
+    out_ref[:, :width] = mixed[:span]
+    out_ref[:, width:] = mixed[span:]
+    sums = jnp.log2(total[:, width:])
+    sum_ref[:, :width] = sums[:span]
+    sum_ref[:, width:] = sums[span:]
+
+
+def attention_forward(query, key, value, order_table, starts):
+    length, wide = query.shape
+    blocks = order_table.shape[0] // 3
+    span = length // blocks
+    padded = jnp.concatenate([value, jnp.ones_like(value)], axis=1)
+    out, sums = pl.pallas_call(
+        attend_kernel,
+        grid=(blocks,),
+        in_specs=[
+            pl.BlockSpec(memory_space=pltpu.SMEM),
+            pl.BlockSpec((span, 1), lambda i: (i, 0)),
+            pl.BlockSpec((span, wide), lambda i: (i, 0)),
+            pl.BlockSpec((length, HEAD_WIDTH), lambda i: (0, 0)),
+            pl.BlockSpec((length, 2 * HEAD_WIDTH), lambda i: (0, 0)),
+        ],
+        out_specs=[
+            pl.BlockSpec((span, wide), lambda i: (i, 0)),
+            pl.BlockSpec((span, wide), lambda i: (i, 0)),
+        ],
+        out_shape=[
+            jax.ShapeDtypeStruct((length, wide), jnp.float32),
+            jax.ShapeDtypeStruct((length, wide), jnp.float32),
+        ],
+        compiler_params=pltpu.CompilerParams(vmem_limit_bytes=40 * 1024 * 1024),
+        cost_estimate=pl.CostEstimate(
+            flops=4 * length * length * wide // 2,
+            bytes_accessed=12 * length * wide,
+            transcendentals=length * length,
+        ),
+        name="attend",
+    )(order_table, starts[:, None], query, key, padded)
+    return out, sums[:, ::HEAD_WIDTH]
+
+
+def attend_back_kernel(
+    order_ref,
+    start_ref,
+    sum_ref,
+    delta_ref,
+    query_ref,
+    grad_ref,
+    key_ref,
+    value_ref,
+    query_grad_ref,
+    key_grad_ref,
+    value_grad_ref,
+):
+    block = pl.program_id(0)
+    blocks = pl.num_programs(0)
+    span = query_ref.shape[0]
+    width = HEAD_WIDTH
+    scale_factor = HEAD_WIDTH ** (-0.5)
+    factor = scale_factor * math.log2(math.e)
+
+    @pl.when(block == 0)
+    def _():
+        key_grad_ref[...] = jnp.zeros_like(key_grad_ref)
+        value_grad_ref[...] = jnp.zeros_like(value_grad_ref)
+
+    query = jnp.concatenate([query_ref[:, :width], query_ref[:, width:]], axis=0)
+    grad = jnp.concatenate([grad_ref[:, :width], grad_ref[:, width:]], axis=0)
+    own = order_ref[block]
+    rows = own * span + lax.broadcasted_iota(jnp.int32, (span, span), 1)
+    columns = lax.broadcasted_iota(jnp.int32, (span, span), 0)
+    starts = start_ref[0]
+    sums = sum_ref[0]
+    delta = delta_ref[0]
+
+    def one_span(turn, total):
+        place = pl.multiple_of(order_ref[blocks + turn] * span, span)
+        here = pl.ds(place, span)
+        keys = key_ref[here, :]
+        scores = lax.dot_general(
+            keys, query, (((1,), (1,)), ((), ())), preferred_element_type=jnp.float32
+        )
+        prob_grad = lax.dot_general(
+            value_ref[here, :], grad, (((1,), (1,)), ((), ())), preferred_element_type=jnp.float32
+        )
+        at = columns + turn * span
+        allowed = (at <= rows) & (at >= starts)
+        allowed = jnp.concatenate([allowed, allowed], axis=1)
+        probs = jnp.where(allowed, jnp.exp2(scores * factor - sums), 0.0)
+        score_grad = (probs * (prob_grad - delta)).astype(jnp.bfloat16)
+        value_grad_ref[here, :] += jnp.dot(
+            probs.astype(jnp.bfloat16), grad, preferred_element_type=jnp.float32
+        )
+        key_grad_ref[here, :] += (
+            jnp.dot(score_grad, query, preferred_element_type=jnp.float32) * scale_factor
+        )
+        return total + lax.dot_general(
+            score_grad, keys, (((0,), (0,)), ((), ())), preferred_element_type=jnp.float32
+        )
+
+    total = lax.fori_loop(
+        order_ref[2 * blocks + block],
+        own + 1,
+        one_span,
+        jnp.zeros((2 * span, width), jnp.float32),
+    )
+    total = total * scale_factor
+    query_grad_ref[:, :width] = total[:span]
+    query_grad_ref[:, width:] = total[span:]
+
+
+def attention_backward(query, key, value, order_table, starts, sums, attended, attended_grad):
+    length, wide = query.shape
+    blocks = order_table.shape[0] // 3
+    span = length // blocks
+    heads = wide // HEAD_WIDTH
+    delta = jnp.sum(
+        (attended * attended_grad.astype(jnp.float32)).reshape(length, heads, HEAD_WIDTH), axis=-1
+    )
+
+    def along_lanes(columns):
+        split = columns.reshape(blocks, span, heads)
+        return split.transpose(0, 2, 1).reshape(blocks, 1, heads * span)
+
+    by_block = pl.BlockSpec((span, wide), lambda i: (i, 0))
+    whole = pl.BlockSpec((length, HEAD_WIDTH), lambda i: (0, 0))
+    lane_row = pl.BlockSpec((1, 1, heads * span), lambda i: (i, 0, 0))
+    return pl.pallas_call(
+        attend_back_kernel,
+        grid=(blocks,),
+        in_specs=[
+            pl.BlockSpec(memory_space=pltpu.SMEM),
+            pl.BlockSpec((1, 1, span), lambda i: (i, 0, 0)),
+            lane_row,
+            lane_row,
+            by_block,
+            by_block,
+            whole,
+            whole,
+        ],
+        out_specs=[by_block, whole, whole],
+        out_shape=[
+            jax.ShapeDtypeStruct((length, wide), jnp.float32),
+            jax.ShapeDtypeStruct((length, HEAD_WIDTH), jnp.float32),
+            jax.ShapeDtypeStruct((length, HEAD_WIDTH), jnp.float32),
+        ],
+        compiler_params=pltpu.CompilerParams(vmem_limit_bytes=40 * 1024 * 1024),
+        cost_estimate=pl.CostEstimate(
+            flops=10 * length * length * wide // 2,
+            bytes_accessed=16 * length * wide,
+            transcendentals=length * length,
+        ),
+        name="attend_back",
+    )(
+        order_table,
+        starts.reshape(blocks, 1, span),
+        along_lanes(sums),
+        along_lanes(delta),
+        query,
+        attended_grad,
+        key,
+        value,
+    )
+
+
+def span_table(segments, span_order, span_length):
+    starts = jnp.sum((segments[None, :] < segments[:, None]).astype(jnp.int32), axis=1)
+    blocks = span_order.shape[0]
+    block_of = jnp.sum(
+        jnp.where(
+            span_order[None, :] == jnp.arange(blocks, dtype=jnp.int32)[:, None],
+            jnp.arange(blocks, dtype=jnp.int32)[None, :],
+            0,
+        ),
+        axis=1,
+    )
+    first = jnp.min(starts.reshape(blocks, span_length), axis=1) // span_length
+    return starts, jnp.concatenate([span_order, block_of, first]).astype(jnp.int32)
+
+
+def head_device(
+    tokens,
+    cotangent,
+    segments,
+    span_order,
+    query_weight,
+    query_moment,
+    query_second,
+    key_value_weight,
+    key_value_first_moment,
+    key_value_second_moment,
+    mixing_weight,
+    mixing_moment,
+    mixing_second,
+    gate_up_weight,
+    gate_up_moment,
+    gate_up_second,
+    down_weight,
+    down_moment,
+    down_second,
+    norm_gains,
+    gain_moment,
+    gain_second,
+):
+    span_length = tokens.shape[1]
+    count = KEY_VALUE_HEADS
+    group = QUERY_HEADS // KEY_VALUE_HEADS
+    wide = group * HEAD_WIDTH
+    ctx_index = lax.axis_index("ctx")
+    attn_gain = norm_gains[:MODEL_WIDTH]
+    mlp_gain = norm_gains[MODEL_WIDTH : 2 * MODEL_WIDTH]
+    query_gain = norm_gains[2 * MODEL_WIDTH : 2 * MODEL_WIDTH + HEAD_WIDTH]
+    key_norm_weight = norm_gains[2 * MODEL_WIDTH + HEAD_WIDTH :]
+
+    tokens_full = gather(tokens[0], "ctx")
+    keyval_pair = pair_columns(key_value_weight.astype(jnp.bfloat16), ctx_index, count)
+    qkv_weight = gather(
+        jnp.concatenate([query_weight.astype(jnp.bfloat16), keyval_pair], axis=1), "dp"
+    )
+    mixing_cols = gather(mixing_weight.astype(jnp.bfloat16), "dp")
+    mixing_rows = lax.all_to_all(mixing_cols, "ctx", 0, 1, tiled=True)
+    gate_up_cols = gather(
+        pair_columns(gate_up_weight.astype(jnp.bfloat16), ctx_index, count), "dp"
+    )
+    down_cols = gather(down_weight.astype(jnp.bfloat16), "dp")
+    down_rows = lax.all_to_all(down_cols, "ctx", 0, 1, tiled=True)
+    cotangent_full = gather(cotangent[0], "ctx")
+
+    offsets = jnp.arange(SEQUENCE_LENGTH, dtype=jnp.int32) % span_length
+    positions = jnp.repeat(span_order[0], span_length) * span_length + offsets
+    cosine_table, sine_table = angles_of(positions)
+    head_fn = functools.partial(
+        head_norms, cosine_table=cosine_table[:, None, :], sine_table=sine_table[:, None, :]
+    )
+
+    normed_one = normalized_input(tokens_full.astype(jnp.float32), attn_gain).astype(jnp.bfloat16)
+    qkv = jnp.dot(normed_one, qkv_weight, preferred_element_type=jnp.float32)
+    query_raw = qkv[:, :wide].reshape(SEQUENCE_LENGTH, group, HEAD_WIDTH)
+    key_raw = qkv[:, wide : wide + HEAD_WIDTH].reshape(SEQUENCE_LENGTH, 1, HEAD_WIDTH)
+    value = qkv[:, wide + HEAD_WIDTH :].astype(jnp.bfloat16)
+    (query_rot, key_rot), heads_back = jax.vjp(
+        head_fn, query_raw, key_raw, query_gain, key_norm_weight
+    )
+    query_rot = query_rot.astype(jnp.bfloat16).reshape(SEQUENCE_LENGTH, wide)
+    key_rot = key_rot[:, 0].astype(jnp.bfloat16)
+    starts, order_table = span_table(segments[0], span_order[0], span_length)
+    attended_wide, sums = attention_forward(query_rot, key_rot, value, order_table, starts)
+    attended = attended_wide.astype(jnp.bfloat16)
+
+    inputs = tokens[0].astype(jnp.float32)
+    middle = inputs + scatter(
+        jnp.dot(attended, mixing_rows, preferred_element_type=jnp.float32), "ctx"
+    )
+    normed_two = normalized_input(middle, mlp_gain).astype(jnp.bfloat16)
+    normed_two_full = gather(normed_two, "ctx")
+    gate_up = jnp.dot(normed_two_full, gate_up_cols, preferred_element_type=jnp.float32)
+    half = gate_up.shape[1] // 2
+
+    def gated(both):
+        return jax.nn.silu(both[:, :half]) * both[:, half:]
+
+    hidden, gated_back = jax.vjp(gated, gate_up)
+    hidden = hidden.astype(jnp.bfloat16)
+    hidden_grad = times_transposed(cotangent_full, down_rows)
+    gate_up_grad = gated_back(hidden_grad)[0].astype(jnp.bfloat16)
+    normed_two_grad = scatter(times_transposed(gate_up_grad, gate_up_cols), "ctx")
+    result = middle + scatter(
+        jnp.dot(hidden, down_rows, preferred_element_type=jnp.float32), "ctx"
+    )
+    block_output = result.astype(jnp.bfloat16)[None]
+
+    unused_norm, norm_two_back = jax.vjp(normalized_input, middle, mlp_gain)
+    middle_part, mlp_gain_grad = norm_two_back(normed_two_grad)
+    middle_grad = cotangent[0].astype(jnp.float32) + middle_part
+    middle_low = gather(middle_grad.astype(jnp.bfloat16), "ctx")
+    attended_grad = times_transposed(middle_low, mixing_rows).astype(jnp.bfloat16)
+
+    def rows_back(gradient):
+        columns = lax.all_to_all(gradient.astype(jnp.bfloat16), "ctx", 1, 0, tiled=True)
+        return scatter(columns, "dp")
+
+    down_total = rows_back(rows_product(hidden, cotangent_full))
+    gate_up_total = unpair_columns(
+        scatter(rows_product(normed_two_full, gate_up_grad), "dp").astype(jnp.bfloat16),
+        ctx_index,
+        count,
+    ).astype(jnp.float32)
+    mixing_total = rows_back(rows_product(attended, middle_low))
+
+    query_rot_grad, key_rot_grad, value_grad = attention_backward(
+        query_rot, key_rot, value, order_table, starts, sums, attended_wide, attended_grad
+    )
+    query_raw_grad, key_raw_grad, query_gain_grad, key_gain_grad = heads_back(
+        (
+            query_rot_grad.reshape(SEQUENCE_LENGTH, group, HEAD_WIDTH),
+            key_rot_grad[:, None, :],
+        )
+    )
+    qkv_grad = jnp.concatenate(
+        [query_raw_grad.reshape(SEQUENCE_LENGTH, wide), key_raw_grad[:, 0], value_grad], axis=1
+    ).astype(jnp.bfloat16)
+    normed_one_grad = scatter(times_transposed(qkv_grad, qkv_weight), "ctx")
+    qkv_total = scatter(rows_product(normed_one, qkv_grad), "dp").astype(jnp.bfloat16)
+    query_total = qkv_total[:, :wide].astype(jnp.float32)
+    keyval_total = unpair_columns(qkv_total[:, wide:], ctx_index, count).astype(jnp.float32)
+    unused_first, norm_one_back = jax.vjp(normalized_input, inputs, attn_gain)
+    input_part, attn_gain_grad = norm_one_back(normed_one_grad)
+    input_grad = (middle_grad + input_part)[None]
+
+    gain_terms = jnp.concatenate([attn_gain_grad, mlp_gain_grad, query_gain_grad, key_gain_grad])
+    gain_total = lax.psum(gain_terms, ("dp", "ctx"))
+    model_rate = 2.0 / math.sqrt(MODEL_WIDTH)
+    mixing_rate = 2.0 / math.sqrt(QUERY_HEADS * HEAD_WIDTH // 32)
+    down_rate = 2.0 / math.sqrt(FF)
+    return (
+        block_output,
+        input_grad,
+        *adamw(query_weight, query_moment, query_second, query_total, model_rate, weight_decay),
+        *adamw(
+            key_value_weight,
+            key_value_first_moment,
+            key_value_second_moment,
+            keyval_total,
+            model_rate,
+            weight_decay,
+        ),
+        *adamw(
+            mixing_weight, mixing_moment, mixing_second, mixing_total, mixing_rate, weight_decay
+        ),
+        *adamw(
+            gate_up_weight, gate_up_moment, gate_up_second, gate_up_total, model_rate, weight_decay
+        ),
+        *adamw(down_weight, down_moment, down_second, down_total, down_rate, weight_decay),
+        *adamw(norm_gains, gain_moment, gain_second, gain_total, gain_rate, 0.0),
+    )
+
+
 def solution(mesh):
     in_specs = (
         P("dp", "ctx", None),
@@ -425,6 +844,8 @@
         P(),
         P(),
     )
+    fits = mesh.shape["ctx"] == KEY_VALUE_HEADS and mesh.shape["dp"] == SEQUENCES
+    per_device = head_device if fits else wide_device
     return jax.shard_map(
         per_device, mesh=mesh, in_specs=in_specs, out_specs=out_specs, check_vma=False
     )

time: 1840 us -> 946 us (0.51)
  waiting for transfers between devices: 1420 us -> 567 us
  matrix products: 185 us -> 64.2 us
  Pallas kernels: 0 us -> 42.1 us
  starting transfers between devices: 1.5 us -> 36.6 us
  blocking collectives: 73.9 us -> 94.9 us
    reduce_scatter x10 -> x8, waiting for transfers between devices: 666 us -> 296 us  [scatter(): lax.psum_scatter(values.astype(jnp.bfloat16), axis_name, scatter_dimensio...]
    all_gather x8 -> x6, waiting for transfers between devices: 555 us -> 209 us  [gather(): return lax.all_gather(values, axis_name, axis=0, tiled=True)]
    unnamed x22 -> x14, waiting for transfers between devices: 198 us -> 1.4 us
    dot_general x11 -> x4, matrix products: 124 us -> 21.6 us  [the longest x1 8.72 us: head_device(): jnp.dot(normed_two_full, gate_up_cols, preferred_element_type=jnp.float32)]
    pallas_call x0 -> x2, Pallas kernels: none -> 42.1 us  [the longest x1 23.8 us: attention_backward(): pl.pallas_call(attend_back_kernel, grid=(blocks,), in_specs=[pl.BlockSpec...]
    all_to_all x0 -> x3, waiting for transfers between devices: none -> 36.4 us  [the longest x2 18.6 us: rows_back(): lax.all_to_all(gradient.astype(jnp.bfloat16), 'ctx', 1, 0, tiled=True)]
    all_to_all x0 -> x1, blocking collectives: none -> 34.2 us  [head_device(): down_rows = lax.all_to_all(down_cols, 'ctx', 0, 1, tiled=True)]
    unnamed x141 -> x154, local copies, waits for them, and re-layouts: 44.2 us -> 14.6 us
  transfers between devices with their start and end apart: 20 -> 25, of which waited for: 18 -> 15; matrix products, arithmetic and copies ran while one was open for 12% -> 14% of each run, Pallas kernels for 0% -> 3%
where the time goes in v1:
time: 946 us; the launch traced here: 942 us
  waiting for transfers between devices  567 us (60%)
  blocking collectives  94.9 us (10%)
  other arithmetic  78.9 us (8%)
  matrix products  64.2 us (7%)
  local copies, waits for them, and re-layouts  43 us (5%)
  Pallas kernels  42.1 us (4%)
  starting transfers between devices  36.6 us (4%)
  between operations  15.2 us (2%)
    reduce_scatter x8, waiting for transfers between devices, scatter(): lax.psum_scatter(values.astype(jnp.bfloat16), axis_name, scatter_dimensio...  296 us
    all_gather x6, waiting for transfers between devices, gather(): return lax.all_gather(values, axis_name, axis=0, tiled=True)  209 us
    psum x1, blocking collectives, head_device(): gain_total = lax.psum(gain_terms, ('dp', 'ctx'))  42.3 us
    all_to_all x1, blocking collectives, head_device(): down_rows = lax.all_to_all(down_cols, 'ctx', 0, 1, tiled=True)  34.2 us
    dot_general x4, matrix products, times_transposed(): lax.dot_general(left_side, right_side, (((1,), (1,)), ((), ())), preferre...  24.1 us
    pallas_call x1, Pallas kernels, attention_backward(): pl.pallas_call(attend_back_kernel, grid=(blocks,), in_specs=[pl.BlockSpec...  23.8 us
    ppermute x2, waiting for transfers between devices, pair_columns(): got_second = lax.ppermute(jnp.where(is_left, high, low), 'ctx', second)  21.7 us
  transfers between devices with their start and end apart: 25, of which 15 were waited for; matrix products, arithmetic and copies ran while one was open for 14% of the time, Pallas kernels for 3%

profile of v1, /device:TPU:0, one launch (start us, length us, event | category | flops | bytes accessed | tf_op | source)
XLA Modules:
  0.0 942.3 jit_solution(12669863740711692144)
XLA Ops:
  16.4 7.6 all_gather.26
  35.4 17.7 %all-to-all-done = bf16[8,256,128]{2,1,0:T(8,128)(2,1)S(1)} async-done(((bf16[8,256,128]{2,1,0:T(8,128)(2,1)}), bf16[8,256,128]{2,1,0:T(8,128)(2,1)S(1)}, u32[]{:S(2)}, u32[]{:S(2)}) %all-to-all-start) | async-done | bytes 524320 | tf_op jit(solution)/shard_map/all_to_all | solution.py:683
  54.2 42.7 %all-gather.17.cloned.1.call-done = bf16[1,2048,1024]{2,1,0:T(8,128)(2,1)} async-done(((bf16[1,256,1024]{2,1,0:T(8,128)(2,1)}), bf16[1,2048,1024]{2,1,0:T(8,128)(2,1)}) %all-gather.17.cloned.1.call-update) | async-done | bytes 4194320 | tf_op jit(solution)/shard_map/all_gather | solution.py:419
  100.0 14.1 %all-gather.9.cloned.1.call-done = bf16[1024,512]{1,0:T(8,128)(2,1)} async-done(((bf16[256,512]{1,0:T(8,128)(2,1)}), bf16[1024,512]{1,0:T(8,128)(2,1)}) %all-gather.9.cloned.1.call-update) | async-done | bytes 1048592 | tf_op jit(solution)/shard_map/all_gather | solution.py:419
  134.4 18.3 %attend.1 = (f32[2048,256]{1,0:T(8,128)S(1)}, f32[2048,256]{1,0:T(8,128)S(1)}) custom-call(s32[24]{0:T(128)S(1)} %pad_add_fusion.2.order_ref, s32[2048,1]{1,0:T(8,128)S(1)} %copy-done.6, bf16[2048,256]{1,0:T(8,128)(2,1)S(1)} %copy-done.4, bf16[2048,128]{1,0:T(8,128)(2,1)S(1)} %maximum_bitcast_fusion.key_ref, bf16[2048,256]{1,0:T(8,128)(2,1)S(1)} %concatenate.37.value_ref), custom_call_target="tpu_custom_call" | custom-call | flops 2147483648 | bytes 6291456 | tf_op jit(solution)/shard_map/attend/pallas_call | solution.py:475
  163.7 21.7 %collective-permute-done.3 = bf16[256,384]{1,0:T(8,128)(2,1)S(1)} collective-permute-done((bf16[256,384]{1,0:T(8,128)(2,1)S(1)}, bf16[256,384]{1,0:T(8,128)(2,1)S(1)}, u32[]{:S(2)}, u32[]{:S(2)}) %collective-permute-start.3) | collective-permute-done | bytes 196640 | tf_op jit(solution)/shard_map/ppermute | solution.py:397
  186.8 66.1 %reduce-scatter.9.cloned.1.call-done = bf16[256,1024]{1,0:T(8,128)(2,1)} async-done(((bf16[2048,1024]{1,0:T(8,128)(2,1)}), bf16[256,1024]{1,0:T(8,128)(2,1)}) %reduce-scatter.9.cloned.1.call-update) | async-done | bytes 524304 | tf_op jit(solution)/shard_map/reduce_scatter | solution.py:423
  258.4 10.8 %all_gather.29 = bf16[3072,128]{1,0:T(8,128)(2,1)S(1)} all-gather(bf16[768,128]{1,0:T(8,128)(2,1)S(1)} %convert_element_type.142), channel_id=1, replica_groups=mesh['dp'=4,'ctx'=8] {'dp'}, dimensions={0}, use_global_device_ids=true | all-gather | bytes 983040 | tf_op jit(solution)/shard_map/all_gather | solution.py:419
  269.1 34.2 %all_to_all.76 = bf16[8,384,128]{2,1,0:T(8,128)(2,1)} all-to-all(bf16[8,384,128]{2,1,0:T(8,128)(2,1)S(1)} %bitcast.133), channel_id=1, replica_groups=mesh['dp'=4,'ctx'=8] {'ctx'}, dimensions={0} | all-to-all | bytes 1572864 | tf_op jit(solution)/shard_map/all_to_all | solution.py:688
  305.6 49.8 %all-gather.11.cloned.1.call-done = bf16[2048,1024]{1,0:T(8,128)(2,1)} async-done(((bf16[256,1024]{1,0:T(8,128)(2,1)}), bf16[2048,1024]{1,0:T(8,128)(2,1)}) %all-gather.11.cloned.1.call-update) | async-done | bytes 4194320 | tf_op jit(solution)/shard_map/all_gather | solution.py:419
  355.4 8.7 fusion.92
  364.1 65.2 %all-gather.19.cloned.1.call-done = bf16[1,2048,1024]{2,1,0:T(8,128)(2,1)} async-done(((bf16[1,256,1024]{2,1,0:T(8,128)(2,1)}), bf16[1,2048,1024]{2,1,0:T(8,128)(2,1)}) %all-gather.19.cloned.1.call-update) | async-done | bytes 4194320 | tf_op jit(solution)/shard_map/all_gather | solution.py:419
  429.3 9.2 fusion.57
  446.4 86.4 %reduce-scatter.13.cloned.1.call-done = bf16[256,1024]{1,0:T(8,128)(2,1)} async-done(((bf16[2048,1024]{1,0:T(8,128)(2,1)}), bf16[256,1024]{1,0:T(8,128)(2,1)}) %reduce-scatter.13.cloned.1.call-update) | async-done | bytes 524304 | tf_op jit(solution)/shard_map/reduce_scatter | solution.py:423
  538.4 8.7 convolution_convert_fusion.5
  557.3 6.6 slice.90
  565.5 18.6 %all-to-all-done.3 = bf16[384,8,128]{2,0,1:T(8,128)(2,1)} async-done(((bf16[384,8,128]{2,0,1:T(8,128)(2,1)}), bf16[384,8,128]{2,0,1:T(8,128)(2,1)}, u32[]{:S(2)}, u32[]{:S(2)}) %all-to-all-start.3) | async-done | bytes 786464 | tf_op jit(solution)/shard_map/all_to_all | solution.py:741
  584.1 36.8 %all-gather.15.cloned.1.call-done = bf16[2048,1024]{1,0:T(8,128)(2,1)} async-done(((bf16[256,1024]{1,0:T(8,128)(2,1)}), bf16[2048,1024]{1,0:T(8,128)(2,1)}) %all-gather.15.cloned.1.call-update) | async-done | bytes 4194320 | tf_op jit(solution)/shard_map/all_gather | solution.py:419
  639.4 23.8 %attend_back.1 = (f32[2048,256]{1,0:T(8,128)S(1)}, f32[2048,128]{1,0:T(8,128)S(1)}, f32[2048,128]{1,0:T(8,128)S(1)}) custom-call(s32[24]{0:T(128)S(1)} %pad_add_fusion.2.order_ref, s32[8,1,256]{2,1,0:T(1,128)S(1)} %bitcast.123, f32[8,1,512]{2,1,0:T(1,128)S(1)} %reshape.321.sum_ref, f32[8,1,512]{2,1,0:T(1,128)S(1)} %reshape.324.delta_ref, ...), custom_call_target="tpu_custom_call" | custom-call | flops 5368709120 | bytes 8388608 | tf_op jit(solution)/shard_map/attend_back/pallas_call | solution.py:590
  663.3 6.1 fusion.39
  732.6 15.2 %reduce-scatter.17.cloned.1.call-done = bf16[256,512]{1,0:T(8,128)(2,1)} async-done(((bf16[1024,512]{1,0:T(8,128)(2,1)}), bf16[256,512]{1,0:T(8,128)(2,1)}) %reduce-scatter.17.cloned.1.call-update) | async-done | bytes 262160 | tf_op jit(solution)/shard_map/reduce_scatter | solution.py:423
  757.8 81.7 %reduce-scatter.15.cloned.1.call-done = bf16[256,1024]{1,0:T(8,128)(2,1)} async-done(((bf16[2048,1024]{1,0:T(8,128)(2,1)}), bf16[256,1024]{1,0:T(8,128)(2,1)}) %reduce-scatter.15.cloned.1.call-update) | async-done | bytes 524304 | tf_op jit(solution)/shard_map/reduce_scatter | solution.py:423
  841.8 42.3 %psum.7 = f32[2304]{0:T(1024)S(1)} all-reduce(f32[2304]{0:T(1024)S(1)} %pad_maximum_fusion.8), channel_id=1, replica_groups=mesh['dp'=4,'ctx'=8] {'dp','ctx'}, use_global_device_ids=true, to_apply=%region_25.26 | all-reduce | flops 2304 | bytes 18432 | tf_op jit(solution)/shard_map/psum | solution.py:773
  886.2 46.2 %reduce-scatter.11.cloned.1.call-done = bf16[256,1024]{1,0:T(8,128)(2,1)} async-done(((bf16[2048,1024]{1,0:T(8,128)(2,1)}), bf16[256,1024]{1,0:T(8,128)(2,1)}) %reduce-scatter.11.cloned.1.call-update) | async-done | bytes 524304 | tf_op jit(solution)/shard_map/reduce_scatter | solution.py:423
  (299 shorter events, 188.3 us)
Async XLA Ops:
  7.2 89.7 %all-gather.17.cloned.1.call-start = ((), (), s32[]{:S(2)}) async-start(), calls=%async_computation.24 | async-start | bytes 4718592 | tf_op jit(solution)/shard_map/all_gather | solution.py:419
  9.0 22.0 %collective-permute-start = (bf16[256,128]{1,0:T(8,128)(2,1)S(1)}, bf16[256,128]{1,0:T(8,128)(2,1)S(1)}, u32[]{:S(2)}, u32[]{:S(2)}) collective-permute-start(bf16[256,128]{1,0:T(8,128)(2,1)S(1)} %get-tuple-element.84), channel_id=1, source_target_pairs={{0,0},{1,2},{2,4},{3,6},{4,1},{5,3},{6,5},{7,7},{8,8},{9,10},{10,1... | collective-permute-start | bytes 196616 | tf_op jit(solution)/shard_map/ppermute | solution.py:396
  9.6 21.4 %collective-permute-start.1 = (bf16[256,128]{1,0:T(8,128)(2,1)S(1)}, bf16[256,128]{1,0:T(8,128)(2,1)S(1)}, u32[]{:S(2)}, u32[]{:S(2)}) collective-permute-start(bf16[256,128]{1,0:T(8,128)(2,1)S(1)} %get-tuple-element.85), channel_id=1, source_target_pairs={{0,1},{1,3},{2,5},{3,7},{4,0},{5,2},{6,4},{7,6},{8,9},{9,11},{10,1... | collective-permute-start | bytes 196616 | tf_op jit(solution)/shard_map/ppermute | solution.py:397
  24.0 29.1 %all-to-all-start = ((bf16[8,256,128]{2,1,0:T(8,128)(2,1)}), bf16[8,256,128]{2,1,0:T(8,128)(2,1)S(1)}, u32[]{:S(2)}, u32[]{:S(2)}) async-start(bf16[8,256,128]{2,1,0:T(8,128)(2,1)} %bitcast.10), calls=%async_computation | async-start | bytes 1048576 | tf_op jit(solution)/shard_map/all_to_all | solution.py:683
  28.7 85.3 %all-gather.9.cloned.1.call-start = ((), (), s32[]{:S(2)}) async-start(), calls=%async_computation.12 | async-start | bytes 1310720 | tf_op jit(solution)/shard_map/all_gather | solution.py:419
  31.8 221.1 %reduce-scatter.9.cloned.1.call-start = ((), (), s32[]{:S(2)}) async-start(), calls=%async_computation.13 | async-start | bytes 4718592 | tf_op jit(solution)/shard_map/reduce_scatter | solution.py:423
  157.4 148.2 %all-gather.13.cloned.1.call-start = ((), (), s32[]{:S(2)}) async-start(), calls=%async_computation.15 | async-start | bytes 1966080 | tf_op jit(solution)/shard_map/all_gather | solution.py:419
  159.5 26.0 %collective-permute-start.3 = (bf16[256,384]{1,0:T(8,128)(2,1)S(1)}, bf16[256,384]{1,0:T(8,128)(2,1)S(1)}, u32[]{:S(2)}, u32[]{:S(2)}) collective-permute-start(bf16[256,384]{1,0:T(8,128)(2,1)S(1)} %get-tuple-element.77), channel_id=1, source_target_pairs={{0,1},{1,3},{2,5},{3,7},{4,0},{5,2},{6,4},{7,6},{8,9},{9,11},{10,1... | collective-permute-start | bytes 589832 | tf_op jit(solution)/shard_map/ppermute | solution.py:397
  186.3 169.1 %all-gather.11.cloned.1.call-start = ((), (), s32[]{:S(2)}) async-start(), calls=%async_computation.14 | async-start | bytes 4718592 | tf_op jit(solution)/shard_map/all_gather | solution.py:419
  257.7 171.6 %all-gather.19.cloned.1.call-start = ((), (), s32[]{:S(2)}) async-start(), calls=%async_computation.25 | async-start | bytes 4718592 | tf_op jit(solution)/shard_map/all_gather | solution.py:419
  258.3 274.5 %reduce-scatter.13.cloned.1.call-start = ((), (), s32[]{:S(2)}) async-start(), calls=%async_computation.17 | async-start | bytes 4718592 | tf_op jit(solution)/shard_map/reduce_scatter | solution.py:423
  446.3 174.6 %all-gather.15.cloned.1.call-start = ((), (), s32[]{:S(2)}) async-start(), calls=%async_computation.18 | async-start | bytes 4718592 | tf_op jit(solution)/shard_map/all_gather | solution.py:419
  538.2 176.6 %reduce-scatter.21.cloned.1.call-start = ((), (), s32[]{:S(2)}) async-start(), calls=%async_computation.22 | async-start | bytes 1966080 | tf_op jit(solution)/shard_map/reduce_scatter | solution.py:423
  552.7 31.4 %all-to-all-start.3 = ((bf16[384,8,128]{2,0,1:T(8,128)(2,1)}), bf16[384,8,128]{2,0,1:T(8,128)(2,1)}, u32[]{:S(2)}, u32[]{:S(2)}) async-start(bf16[384,8,128]{2,0,1:T(8,128)(2,1)} %bitcast.131), calls=%async_computation.10 | async-start | bytes 1572864 | tf_op jit(solution)/shard_map/all_to_all | solution.py:741
  557.2 164.7 %reduce-scatter.23.cloned.1.call-start = ((), (), s32[]{:S(2)}) async-start(), calls=%async_computation.23 | async-start | bytes 983040 | tf_op jit(solution)/shard_map/reduce_scatter | solution.py:423
  678.1 18.6 %all-to-all-start.2 = ((bf16[256,8,128]{2,0,1:T(8,128)(2,1)}), bf16[256,8,128]{2,0,1:T(8,128)(2,1)}, u32[]{:S(2)}, u32[]{:S(2)}) async-start(bf16[256,8,128]{2,0,1:T(8,128)(2,1)} %bitcast.120), calls=%async_computation.7 | async-start | bytes 1048576 | tf_op jit(solution)/shard_map/all_to_all | solution.py:741
  682.2 48.1 %reduce-scatter.19.cloned.1.call-start = ((), (), s32[]{:S(2)}) async-start(), calls=%async_computation.21 | async-start | bytes 655360 | tf_op jit(solution)/shard_map/reduce_scatter | solution.py:423
  696.7 51.1 %reduce-scatter.17.cloned.1.call-start = ((), (), s32[]{:S(2)}) async-start(), calls=%async_computation.20 | async-start | bytes 1310720 | tf_op jit(solution)/shard_map/reduce_scatter | solution.py:423
  704.1 135.5 %reduce-scatter.15.cloned.1.call-start = ((), (), s32[]{:S(2)}) async-start(), calls=%async_computation.19 | async-start | bytes 4718592 | tf_op jit(solution)/shard_map/reduce_scatter | solution.py:423
  708.6 223.7 %reduce-scatter.11.cloned.1.call-start = ((), (), s32[]{:S(2)}) async-start(), calls=%async_computation.16 | async-start | bytes 4718592 | tf_op jit(solution)/shard_map/reduce_scatter | solution.py:423
  716.7 7.6 collective-permute-start.6
  718.3 8.6 collective-permute-start.7
  748.7 7.0 collective-permute-start.4
  749.4 7.4 collective-permute-start.5
  (78 other events, 2806.2 us)
Sparse Core Ops, SparseCore 0:
  10.2 86.6 all-gather.16
  99.0 14.9 all-gather.8
  157.5 95.2 reduce-scatter.8
  254.9 21.0 all-gather.12
  278.7 76.6 all-gather.10
  357.6 71.6 all-gather.18
  446.4 86.3 reduce-scatter.12
  538.3 82.5 all-gather.14
  623.4 26.4 reduce-scatter.20
  652.5 23.2 reduce-scatter.22
  696.8 22.9 reduce-scatter.18
  722.9 24.8 reduce-scatter.16
  751.4 88.0 reduce-scatter.14
  843.5 88.8 reduce-scatter.10

commit v2 on v1

--- a/solution.py
+++ b/solution.py
@@ -423,6 +423,23 @@
     return lax.psum_scatter(
         values.astype(jnp.bfloat16), axis_name, scatter_dimension=0, tiled=True
     ).astype(jnp.float32)
+
+
+def rows_from_all(values, axis_name):
+    count = lax.axis_size(axis_name)
+    copies = jnp.broadcast_to(values[None], (count,) + values.shape)
+    return lax.all_to_all(copies, axis_name, 0, 0).reshape((-1,) + values.shape[1:])
+
+
+def rows_summed(values, axis_name):
+    count = lax.axis_size(axis_name)
+    split = values.astype(jnp.bfloat16).reshape((count, -1) + values.shape[1:])
+    return jnp.sum(lax.all_to_all(split, axis_name, 0, 0).astype(jnp.float32), axis=0)
+
+
+def total_over(values, axis_name):
+    count = lax.axis_size(axis_name)
+    return jnp.sum(rows_from_all(values[None], axis_name).reshape((count,) + values.shape), axis=0)
 
 
 def attend_kernel(order_ref, start_ref, query_ref, key_ref, value_ref, out_ref, sum_ref):
@@ -676,17 +693,18 @@
 
     tokens_full = gather(tokens[0], "ctx")
     keyval_pair = pair_columns(key_value_weight.astype(jnp.bfloat16), ctx_index, count)
-    qkv_weight = gather(
+    qkv_weight = rows_from_all(
         jnp.concatenate([query_weight.astype(jnp.bfloat16), keyval_pair], axis=1), "dp"
     )
-    mixing_cols = gather(mixing_weight.astype(jnp.bfloat16), "dp")
+    mixing_cols = rows_from_all(mixing_weight.astype(jnp.bfloat16), "dp")
     mixing_rows = lax.all_to_all(mixing_cols, "ctx", 0, 1, tiled=True)
-    gate_up_cols = gather(
+    gate_up_cols = rows_from_all(
         pair_columns(gate_up_weight.astype(jnp.bfloat16), ctx_index, count), "dp"
     )
-    down_cols = gather(down_weight.astype(jnp.bfloat16), "dp")
+    down_cols = rows_from_all(down_weight.astype(jnp.bfloat16), "dp")
     down_rows = lax.all_to_all(down_cols, "ctx", 0, 1, tiled=True)
-    cotangent_full = gather(cotangent[0], "ctx")
+    own_cotangent, tokens_full = lax.optimization_barrier((cotangent[0], tokens_full))
+    cotangent_full = gather(own_cotangent, "ctx")
 
     offsets = jnp.arange(SEQUENCE_LENGTH, dtype=jnp.int32) % span_length
     positions = jnp.repeat(span_order[0], span_length) * span_length + offsets
@@ -710,9 +728,11 @@
     attended = attended_wide.astype(jnp.bfloat16)
 
     inputs = tokens[0].astype(jnp.float32)
-    middle = inputs + scatter(
-        jnp.dot(attended, mixing_rows, preferred_element_type=jnp.float32), "ctx"
-    )
+    mixed = jnp.dot(attended, mixing_rows, preferred_element_type=jnp.float32).astype(jnp.bfloat16)
+    mixed, cotangent_full, gate_up_cols, down_rows = lax.optimization_barrier(
+        (mixed, cotangent_full, gate_up_cols, down_rows)
+    )
+    middle = inputs + scatter(mixed, "ctx")
     normed_two = normalized_input(middle, mlp_gain).astype(jnp.bfloat16)
     normed_two_full = gather(normed_two, "ctx")
     gate_up = jnp.dot(normed_two_full, gate_up_cols, preferred_element_type=jnp.float32)
@@ -726,24 +746,24 @@
     hidden_grad = times_transposed(cotangent_full, down_rows)
     gate_up_grad = gated_back(hidden_grad)[0].astype(jnp.bfloat16)
     normed_two_grad = scatter(times_transposed(gate_up_grad, gate_up_cols), "ctx")
-    result = middle + scatter(
-        jnp.dot(hidden, down_rows, preferred_element_type=jnp.float32), "ctx"
-    )
-    block_output = result.astype(jnp.bfloat16)[None]
-
     unused_norm, norm_two_back = jax.vjp(normalized_input, middle, mlp_gain)
     middle_part, mlp_gain_grad = norm_two_back(normed_two_grad)
     middle_grad = cotangent[0].astype(jnp.float32) + middle_part
     middle_low = gather(middle_grad.astype(jnp.bfloat16), "ctx")
+    hidden_out = jnp.dot(hidden, down_rows, preferred_element_type=jnp.float32)
+    hidden_out, middle_low = lax.optimization_barrier(
+        (hidden_out.astype(jnp.bfloat16), middle_low)
+    )
+    hidden_sum = scatter(hidden_out, "ctx")
     attended_grad = times_transposed(middle_low, mixing_rows).astype(jnp.bfloat16)
 
     def rows_back(gradient):
         columns = lax.all_to_all(gradient.astype(jnp.bfloat16), "ctx", 1, 0, tiled=True)
-        return scatter(columns, "dp")
+        return rows_summed(columns, "dp")
 
     down_total = rows_back(rows_product(hidden, cotangent_full))
     gate_up_total = unpair_columns(
-        scatter(rows_product(normed_two_full, gate_up_grad), "dp").astype(jnp.bfloat16),
+        rows_summed(rows_product(normed_two_full, gate_up_grad), "dp").astype(jnp.bfloat16),
         ctx_index,
         count,
     ).astype(jnp.float32)
@@ -761,16 +781,24 @@
     qkv_grad = jnp.concatenate(
         [query_raw_grad.reshape(SEQUENCE_LENGTH, wide), key_raw_grad[:, 0], value_grad], axis=1
     ).astype(jnp.bfloat16)
-    normed_one_grad = scatter(times_transposed(qkv_grad, qkv_weight), "ctx")
-    qkv_total = scatter(rows_product(normed_one, qkv_grad), "dp").astype(jnp.bfloat16)
+    normed_one_part = times_transposed(qkv_grad, qkv_weight)
+    attn_gain_grad = jax.vjp(
+        lambda gain: normalized_input(tokens_full.astype(jnp.float32), gain), attn_gain
+    )[1](normed_one_part)[0]
+    normed_one_low, hidden_sum = lax.optimization_barrier(
+        (normed_one_part.astype(jnp.bfloat16), hidden_sum)
+    )
+    block_output = (middle + hidden_sum).astype(jnp.bfloat16)[None]
+    normed_one_grad = scatter(normed_one_low, "ctx")
+    qkv_total = rows_summed(rows_product(normed_one, qkv_grad), "dp").astype(jnp.bfloat16)
     query_total = qkv_total[:, :wide].astype(jnp.float32)
     keyval_total = unpair_columns(qkv_total[:, wide:], ctx_index, count).astype(jnp.float32)
     unused_first, norm_one_back = jax.vjp(normalized_input, inputs, attn_gain)
-    input_part, attn_gain_grad = norm_one_back(normed_one_grad)
+    input_part = norm_one_back(normed_one_grad)[0]
     input_grad = (middle_grad + input_part)[None]
 
     gain_terms = jnp.concatenate([attn_gain_grad, mlp_gain_grad, query_gain_grad, key_gain_grad])
-    gain_total = lax.psum(gain_terms, ("dp", "ctx"))
+    gain_total = total_over(total_over(gain_terms, "ctx"), "dp")
     model_rate = 2.0 / math.sqrt(MODEL_WIDTH)
     mixing_rate = 2.0 / math.sqrt(QUERY_HEADS * HEAD_WIDTH // 32)
     down_rate = 2.0 / math.sqrt(FF)

time: 946 us -> 840 us (0.89)
  blocking collectives: 94.9 us -> 0 us
  waiting for transfers between devices: 567 us -> 489 us
  starting transfers between devices: 36.6 us -> 91.4 us
    reduce_scatter x8 -> x4, waiting for transfers between devices: 296 us -> 181 us  [scatter(): lax.psum_scatter(values.astype(jnp.bfloat16), axis_name, scatter_dimensio...]
    all_to_all x0 -> x11, waiting for transfers between devices: none -> 77.8 us  [the longest x1 30 us: head_device(): down_rows = lax.all_to_all(down_cols, 'ctx', 0, 1, tiled=True)]
    all_to_all x0 -> x11, starting transfers between devices: none -> 43.9 us  [the longest x6 23.9 us: rows_from_all(): lax.all_to_all(copies, axis_name, 0, 0).reshape((-1,) + values.shape[1:])]
    psum x1 -> x0, blocking collectives: 42.3 us -> none  [head_device(): gain_total = lax.psum(gain_terms, ('dp', 'ctx'))]
    all_to_all x1 -> x0, blocking collectives: 34.2 us -> none  [head_device(): down_rows = lax.all_to_all(down_cols, 'ctx', 0, 1, tiled=True)]
    ppermute x2, waiting for transfers between devices: 21.7 us -> 0.01 us  [pair_columns(): got_second = lax.ppermute(jnp.where(is_left, high, low), 'ctx', second)]
    all_gather x6 -> x4, waiting for transfers between devices: 209 us -> 188 us  [gather(): return lax.all_gather(values, axis_name, axis=0, tiled=True)]
    all_gather x2 -> x0, blocking collectives: 18.4 us -> none  [gather(): return lax.all_gather(values, axis_name, axis=0, tiled=True)]
  transfers between devices with their start and end apart: 25 -> 30, of which waited for: 15 -> 17; matrix products, arithmetic and copies ran while one was open for 14% -> 17% of each run, Pallas kernels for 3% -> 5%
where the time goes in v2:
time: 840 us; the launch traced here: 832 us
  waiting for transfers between devices  489 us (58%)
  starting transfers between devices  91.4 us (11%)
  other arithmetic  77.4 us (9%)
  matrix products  64.5 us (8%)
  local copies, waits for them, and re-layouts  52.4 us (6%)
  Pallas kernels  42.1 us (5%)
  between operations  15.7 us (2%)
    all_gather x4, waiting for transfers between devices, gather(): return lax.all_gather(values, axis_name, axis=0, tiled=True)  188 us
    reduce_scatter x4, waiting for transfers between devices, scatter(): lax.psum_scatter(values.astype(jnp.bfloat16), axis_name, scatter_dimensio...  181 us
    all_to_all x2, waiting for transfers between devices, rows_back(): lax.all_to_all(gradient.astype(jnp.bfloat16), 'ctx', 1, 0, tiled=True)  30.6 us
    all_to_all x1, waiting for transfers between devices, head_device(): down_rows = lax.all_to_all(down_cols, 'ctx', 0, 1, tiled=True)  30 us
    all_to_all x4, waiting for transfers between devices, rows_summed(): lax.all_to_all(split, axis_name, 0, 0).astype(jnp.float32)  28.2 us
    all_to_all x6, starting transfers between devices, rows_from_all(): lax.all_to_all(copies, axis_name, 0, 0).reshape((-1,) + values.shape[1:])  23.9 us
    pallas_call x1, Pallas kernels, attention_backward(): pl.pallas_call(attend_back_kernel, grid=(blocks,), in_specs=[pl.BlockSpec...  23.8 us
    dot_general x4, matrix products, times_transposed(): lax.dot_general(left_side, right_side, (((1,), (1,)), ((), ())), preferre...  22.8 us
  transfers between devices with their start and end apart: 30, of which 17 were waited for; matrix products, arithmetic and copies ran while one was open for 17% of the time, Pallas kernels for 5%

profile of v2, /device:TPU:0, one launch (start us, length us, event | category | flops | bytes accessed | tf_op | source)
XLA Modules:
  0.0 832.1 jit_solution(5117472163506960662)
XLA Ops:
  40.4 6.6 all-to-all-start.2
  50.1 47.8 %all-gather.12.cloned.1.call-done = bf16[1,2048,1024]{2,1,0:T(8,128)(2,1)} async-done(((bf16[1,256,1024]{2,1,0:T(8,128)(2,1)}), bf16[1,2048,1024]{2,1,0:T(8,128)(2,1)}) %all-gather.12.cloned.1.call-update) | async-done | bytes 4194320 | tf_op jit(solution)/shard_map/all_gather | solution.py:419
  107.2 30.0 %all-to-all-done.5 = bf16[8,384,128]{2,1,0:T(8,128)(2,1)S(1)} async-done(((bf16[8,384,128]{2,1,0:T(8,128)(2,1)}), bf16[8,384,128]{2,1,0:T(8,128)(2,1)S(1)}, u32[]{:S(2)}, u32[]{:S(2)}) %all-to-all-start.5) | async-done | bytes 786464 | tf_op jit(solution)/shard_map/all_to_all | solution.py:705
  148.8 8.2 all-to-all-done
  187.4 18.3 %attend.1 = (f32[2048,256]{1,0:T(8,128)S(1)}, f32[2048,256]{1,0:T(8,128)S(1)}) custom-call(s32[24]{0:T(128)S(1)} %pad_add_fusion.2.order_ref, s32[2048,1]{1,0:T(8,128)S(1)} %copy.108.start_ref, bf16[2048,256]{1,0:T(8,128)(2,1)S(1)} %copy-done.5, bf16[2048,128]{1,0:T(8,128)(2,1)S(1)} %maximum_bitcast_fusion.key_ref, bf16[2048,256]{1,0:T(8,128)(2,1)S(1)} %concatenate.37.value_ref), custom_call_target="tpu_custom_call" | custom-call | flops 2147483648 | bytes 6291456 | tf_op jit(solution)/shard_map/attend/pallas_call | solution.py:492
  210.6 88.3 %reduce-scatter.5.cloned.1.call-done = bf16[256,1024]{1,0:T(8,128)(2,1)} async-done(((bf16[2048,1024]{1,0:T(8,128)(2,1)}), bf16[256,1024]{1,0:T(8,128)(2,1)}) %reduce-scatter.5.cloned.1.call-update) | async-done | bytes 524304 | tf_op jit(solution)/shard_map/reduce_scatter | solution.py:423
  302.5 73.1 %all-gather.8.cloned.1.call-done = bf16[2048,1024]{1,0:T(8,128)(2,1)} async-done(((bf16[256,1024]{1,0:T(8,128)(2,1)}), bf16[2048,1024]{1,0:T(8,128)(2,1)}) %all-gather.8.cloned.1.call-update) | async-done | bytes 4194320 | tf_op jit(solution)/shard_map/all_gather | solution.py:419
  388.7 6.5 convolution_convert_fusion.2
  395.3 86.2 %reduce-scatter.7.cloned.1.call-done = bf16[256,1024]{1,0:T(8,128)(2,1)} async-done(((bf16[2048,1024]{1,0:T(8,128)(2,1)}), bf16[256,1024]{1,0:T(8,128)(2,1)}) %reduce-scatter.7.cloned.1.call-update) | async-done | bytes 524304 | tf_op jit(solution)/shard_map/reduce_scatter | solution.py:423
  486.3 6.0 convolution_convert_fusion
  492.3 67.3 %all-gather.10.cloned.1.call-done = bf16[2048,1024]{1,0:T(8,128)(2,1)} async-done(((bf16[256,1024]{1,0:T(8,128)(2,1)}), bf16[2048,1024]{1,0:T(8,128)(2,1)}) %all-gather.10.cloned.1.call-update) | async-done | bytes 4194320 | tf_op jit(solution)/shard_map/all_gather | solution.py:419
  559.9 6.6 slice.87
  586.2 23.8 %attend_back.1 = (f32[2048,256]{1,0:T(8,128)S(1)}, f32[2048,128]{1,0:T(8,128)S(1)}, f32[2048,128]{1,0:T(8,128)S(1)}) custom-call(s32[24]{0:T(128)S(1)} %pad_add_fusion.2.order_ref, s32[8,1,256]{2,1,0:T(1,128)S(1)} %bitcast.111, f32[8,1,512]{2,1,0:T(1,128)S(1)} %reshape.359.sum_ref, f32[8,1,512]{2,1,0:T(1,128)S(1)} %reshape.362.delta_ref, ...), custom_call_target="tpu_custom_call" | custom-call | flops 5368709120 | bytes 8388608 | tf_op jit(solution)/shard_map/attend_back/pallas_call | solution.py:607
  636.1 6.4 fusion.3
  642.5 6.9 reduce-scatter.9.cloned.1.call-done
  651.6 8.8 %convolution_convert_fusion.4 = bf16[1024,768]{1,0:T(8,128)(2,1)} fusion(bf16[2048,1024]{1,0:T(8,128)(2,1)} %all-gather.8.cloned.1.call-done, f32[2048,384]{1,0:T(8,128)} %copy-done.70, f32[2048,384]{1,0:T(8,128)} %copy-done.69), kind=kOutput, calls=%fused_computation.32 | convolution fusion | flops 3225157632 | bytes 12058624 | tf_op jit(solution)/shard_map/dot_general | solution.py:80
  670.2 14.6 %all-to-all-done.9 = bf16[4,256,768]{2,1,0:T(8,128)(2,1)} async-done(((bf16[4,256,768]{2,1,0:T(8,128)(2,1)}), bf16[4,256,768]{2,1,0:T(8,128)(2,1)}, u32[]{:S(2)}, u32[]{:S(2)}) %all-to-all-start.9) | async-done | bytes 1572896 | tf_op jit(solution)/shard_map/all_to_all | solution.py:437
  689.2 24.7 %all-to-all-done.10 = bf16[384,8,128]{2,0,1:T(8,128)(2,1)S(1)} async-done(((bf16[384,8,128]{2,0,1:T(8,128)(2,1)}), bf16[384,8,128]{2,0,1:T(8,128)(2,1)S(1)}, u32[]{:S(2)}, u32[]{:S(2)}) %all-to-all-start.10) | async-done | bytes 786464 | tf_op jit(solution)/shard_map/all_to_all | solution.py:761
  732.4 9.7 %collective-permute-done.7 = bf16[256,384]{1,0:T(8,128)(2,1)S(1)} collective-permute-done((bf16[256,384]{1,0:T(8,128)(2,1)S(1)}, bf16[256,384]{1,0:T(8,128)(2,1)S(1)}, u32[]{:S(2)}, u32[]{:S(2)}) %collective-permute-start.7) | collective-permute-done | bytes 196640 | tf_op jit(solution)/shard_map/ppermute | solution.py:410
  747.2 6.6 convolution_convert_fusion.5
  764.7 7.7 all-to-all-done.6
  772.4 13.9 %all-to-all-start.7 = ((bf16[256,8,128]{2,0,1:T(8,128)(2,1)}), bf16[256,8,128]{2,0,1:T(8,128)(2,1)S(1)}, u32[]{:S(2)}, u32[]{:S(2)}) async-start(bf16[256,8,128]{2,0,1:T(8,128)(2,1)} %bitcast.108), calls=%async_computation.11 | async-start | bytes 1048576 | tf_op jit(solution)/shard_map/all_to_all | solution.py:761
  796.8 5.9 all-to-all-done.7
  810.7 5.9 all-to-all-done.8
  (302 shorter events, 236.5 us)
Async XLA Ops:
  7.2 90.7 %all-gather.12.cloned.1.call-start = ((), (), s32[]{:S(2)}) async-start(), calls=%async_computation.25 | async-start | bytes 4718592 | tf_op jit(solution)/shard_map/all_gather | solution.py:419
  15.7 90.6 %collective-permute-start = (bf16[256,128]{1,0:T(8,128)(2,1)}, bf16[256,128]{1,0:T(8,128)(2,1)S(1)}, u32[]{:S(2)}, u32[]{:S(2)}) collective-permute-start(bf16[256,128]{1,0:T(8,128)(2,1)} %get-tuple-element.104), channel_id=1, source_target_pairs={{0,0},{1,2},{2,4},{3,6},{4,1},{5,3},{6,5},{7,7},{8,8},{9,10},{10,1... | collective-permute-start | bytes 196616 | tf_op jit(solution)/shard_map/ppermute | solution.py:396
  17.3 89.0 %collective-permute-start.1 = (bf16[256,128]{1,0:T(8,128)(2,1)}, bf16[256,128]{1,0:T(8,128)(2,1)}, u32[]{:S(2)}, u32[]{:S(2)}) collective-permute-start(bf16[256,128]{1,0:T(8,128)(2,1)} %get-tuple-element.105), channel_id=1, source_target_pairs={{0,1},{1,3},{2,5},{3,7},{4,0},{5,2},{6,4},{7,6},{8,9},{9,11},{10,1... | collective-permute-start | bytes 196616 | tf_op jit(solution)/shard_map/ppermute | solution.py:397
  24.4 15.9 %all-to-all-start.4 = ((bf16[4,768,128]{2,1,0:T(8,128)(2,1)}), bf16[4,768,128]{2,1,0:T(8,128)(2,1)}, u32[]{:S(2)}, u32[]{:S(2)}) async-start(bf16[4,768,128]{2,1,0:T(8,128)(2,1)} %broadcast_in_dim.49), calls=%async_computation.4 | async-start | bytes 1572864 | tf_op jit(solution)/shard_map/all_to_all | solution.py:431
  29.4 113.1 %collective-permute-start.2 = (bf16[256,384]{1,0:T(8,128)(2,1)}, bf16[256,384]{1,0:T(8,128)(2,1)S(1)}, u32[]{:S(2)}, u32[]{:S(2)}) collective-permute-start(bf16[256,384]{1,0:T(8,128)(2,1)} %get-tuple-element.96), channel_id=1, source_target_pairs={{0,0},{1,2},{2,4},{3,6},{4,1},{5,3},{6,5},{7,7},{8,8},{9,10},{10,1... | collective-permute-start | bytes 589832 | tf_op jit(solution)/shard_map/ppermute | solution.py:396
  31.0 111.5 %collective-permute-start.3 = (bf16[256,384]{1,0:T(8,128)(2,1)}, bf16[256,384]{1,0:T(8,128)(2,1)}, u32[]{:S(2)}, u32[]{:S(2)}) collective-permute-start(bf16[256,384]{1,0:T(8,128)(2,1)} %get-tuple-element.97), channel_id=1, source_target_pairs={{0,1},{1,3},{2,5},{3,7},{4,0},{5,2},{6,4},{7,6},{8,9},{9,11},{10,1... | collective-permute-start | bytes 589832 | tf_op jit(solution)/shard_map/ppermute | solution.py:397
  40.4 58.1 %all-to-all-start.2 = ((bf16[8,256,128]{2,1,0:T(8,128)(2,1)}), bf16[8,256,128]{2,1,0:T(8,128)(2,1)S(1)}, u32[]{:S(2)}, u32[]{:S(2)}) async-start(bf16[8,256,128]{2,1,0:T(8,128)(2,1)} %bitcast.11), calls=%async_computation.2 | async-start | bytes 1048576 | tf_op jit(solution)/shard_map/all_to_all | solution.py:700
  47.0 163.5 %all-gather.6.cloned.1.call-start = ((), (), s32[]{:S(2)}) async-start(), calls=%async_computation.18 | async-start | bytes 4718592 | tf_op jit(solution)/shard_map/all_gather | solution.py:419
  98.4 38.8 %all-to-all-start.5 = ((bf16[8,384,128]{2,1,0:T(8,128)(2,1)}), bf16[8,384,128]{2,1,0:T(8,128)(2,1)S(1)}, u32[]{:S(2)}, u32[]{:S(2)}) async-start(bf16[8,384,128]{2,1,0:T(8,128)(2,1)} %bitcast.15), calls=%async_computation.5 | async-start | bytes 1572864 | tf_op jit(solution)/shard_map/all_to_all | solution.py:705
  138.2 18.8 %all-to-all-start = ((bf16[4,256,512]{2,1,0:T(8,128)(2,1)}), bf16[4,256,512]{2,1,0:T(8,128)(2,1)}, u32[]{:S(2)}, u32[]{:S(2)}) async-start(bf16[4,256,512]{2,1,0:T(8,128)(2,1)} %broadcast_in_dim.45), calls=%async_computation | async-start | bytes 2097152 | tf_op jit(solution)/shard_map/all_to_all | solution.py:431
  158.3 52.2 %all-to-all-start.3 = ((bf16[4,256,768]{2,1,0:T(8,128)(2,1)}), bf16[4,256,768]{2,1,0:T(8,128)(2,1)}, u32[]{:S(2)}, u32[]{:S(2)}) async-start(bf16[4,256,768]{2,1,0:T(8,128)(2,1)} %broadcast_in_dim.48), calls=%async_computation.3 | async-start | bytes 3145728 | tf_op jit(solution)/shard_map/all_to_all | solution.py:431
  162.7 136.2 %reduce-scatter.5.cloned.1.call-start = ((), (), s32[]{:S(2)}) async-start(), calls=%async_computation.19 | async-start | bytes 4718592 | tf_op jit(solution)/shard_map/reduce_scatter | solution.py:423
  210.5 165.1 %all-gather.8.cloned.1.call-start = ((), (), s32[]{:S(2)}) async-start(), calls=%async_computation.20 | async-start | bytes 4718592 | tf_op jit(solution)/shard_map/all_gather | solution.py:419
  302.3 179.3 %reduce-scatter.7.cloned.1.call-start = ((), (), s32[]{:S(2)}) async-start(), calls=%async_computation.21 | async-start | bytes 4718592 | tf_op jit(solution)/shard_map/reduce_scatter | solution.py:423
  395.2 164.3 %all-gather.10.cloned.1.call-start = ((), (), s32[]{:S(2)}) async-start(), calls=%async_computation.22 | async-start | bytes 4718592 | tf_op jit(solution)/shard_map/all_gather | solution.py:419
  486.2 163.2 %reduce-scatter.9.cloned.1.call-start = ((), (), s32[]{:S(2)}) async-start(), calls=%async_computation.23 | async-start | bytes 4718592 | tf_op jit(solution)/shard_map/reduce_scatter | solution.py:423
  559.6 260.2 %reduce-scatter.11.cloned.1.call-start = ((), (), s32[]{:S(2)}) async-start(), calls=%async_computation.24 | async-start | bytes 4718592 | tf_op jit(solution)/shard_map/reduce_scatter | solution.py:423
  660.3 24.5 %all-to-all-start.9 = ((bf16[4,256,768]{2,1,0:T(8,128)(2,1)}), bf16[4,256,768]{2,1,0:T(8,128)(2,1)}, u32[]{:S(2)}, u32[]{:S(2)}) async-start(bf16[4,256,768]{2,1,0:T(8,128)(2,1)} %bitcast.129), calls=%async_computation.13 | async-start | bytes 3145728 | tf_op jit(solution)/shard_map/all_to_all | solution.py:437
  684.8 29.1 %all-to-all-start.10 = ((bf16[384,8,128]{2,0,1:T(8,128)(2,1)}), bf16[384,8,128]{2,0,1:T(8,128)(2,1)S(1)}, u32[]{:S(2)}, u32[]{:S(2)}) async-start(bf16[384,8,128]{2,0,1:T(8,128)(2,1)} %bitcast.126), calls=%async_computation.14 | async-start | bytes 1572864 | tf_op jit(solution)/shard_map/all_to_all | solution.py:761
  725.3 17.9 %all-to-all-start.11 = ((bf16[4,768,128]{2,1,0:T(8,128)(2,1)}), bf16[4,768,128]{2,1,0:T(8,128)(2,1)S(1)}, u32[]{:S(2)}, u32[]{:S(2)}) async-start(bf16[4,768,128]{2,1,0:T(8,128)(2,1)} %bitcast.125), calls=%async_computation.15 | async-start | bytes 1572864 | tf_op jit(solution)/shard_map/all_to_all | solution.py:437
  754.4 18.0 %all-to-all-start.6 = ((bf16[4,256,512]{2,1,0:T(8,128)(2,1)}), bf16[4,256,512]{2,1,0:T(8,128)(2,1)S(1)}, u32[]{:S(2)}, u32[]{:S(2)}) async-start(bf16[4,256,512]{2,1,0:T(8,128)(2,1)} %bitcast.130), calls=%async_computation.10 | async-start | bytes 2097152 | tf_op jit(solution)/shard_map/all_to_all | solution.py:437
  772.4 30.3 %all-to-all-start.7 = ((bf16[256,8,128]{2,0,1:T(8,128)(2,1)}), bf16[256,8,128]{2,0,1:T(8,128)(2,1)S(1)}, u32[]{:S(2)}, u32[]{:S(2)}) async-start(bf16[256,8,128]{2,0,1:T(8,128)(2,1)} %bitcast.108), calls=%async_computation.11 | async-start | bytes 1048576 | tf_op jit(solution)/shard_map/all_to_all | solution.py:761
  790.3 17.5 %collective-permute-start.4 = (bf16[256,128]{1,0:T(8,128)(2,1)}, bf16[256,128]{1,0:T(8,128)(2,1)S(1)}, u32[]{:S(2)}, u32[]{:S(2)}) collective-permute-start(bf16[256,128]{1,0:T(8,128)(2,1)} %get-tuple-element.98), channel_id=1, source_target_pairs={{0,0},{2,1},{4,2},{6,3},{1,4},{3,5},{5,6},{7,7},{8,8},{10,9},{12,1... | collective-permute-start | bytes 196616 | tf_op jit(solution)/shard_map/ppermute | solution.py:409
  791.8 16.0 %collective-permute-start.5 = (bf16[256,128]{1,0:T(8,128)(2,1)S(1)}, bf16[256,128]{1,0:T(8,128)(2,1)}, u32[]{:S(2)}, u32[]{:S(2)}) collective-permute-start(bf16[256,128]{1,0:T(8,128)(2,1)S(1)} %get-tuple-element.99), channel_id=1, source_target_pairs={{1,0},{3,1},{5,2},{7,3},{0,4},{2,5},{4,6},{6,7},{9,8},{11,9},{13,1... | collective-permute-start | bytes 196616 | tf_op jit(solution)/shard_map/ppermute | solution.py:410
  (78 other events, 1397.9 us)
Sparse Core Ops, SparseCore 0:
  10.2 87.6 all-gather.11
  100.0 84.0 all-gather.5
  210.6 88.1 reduce-scatter.4
  302.4 73.1 all-gather.7
  395.4 86.1 reduce-scatter.6
  486.4 73.1 all-gather.9
  563.2 86.1 reduce-scatter.8
  653.5 105.4 reduce-scatter.10
